TPU v7x, 128 devices: a whole 4x4x4 slice. The times are simulated.
128 devices in a mesh: section: 2 (over core), ctx: 16 (over x, y), fsdp: 4 (over z).
Axes of the slice: x: 4, y: 4, z: 4, core: 2. Of those that a mesh axis runs over, the one named last changes fastest.
Arguments:
- inputs: bfloat16 [4, 4, 1024, 576], P(None, 'fsdp', 'ctx'), may hold values from -6 to 6
- piece_order: int32 [4, 4, 32], P(None, 'fsdp'), may hold values from 0 to 31, as said below
- cotangent: bfloat16 [4, 4, 1024, 576], P(None, 'fsdp', 'ctx'), may hold values from -6 to 6
- gain_attn: bfloat16 [2, 576], P('section', 'fsdp'), may hold values from 0.5 to 1.5
- w_query: bfloat16 [2, 576, 576], P('section', 'fsdp'), may hold values from -0.25 to 0.25
- key_weight: bfloat16 [2, 576, 192], P('section', 'fsdp'), may hold values from -0.25 to 0.25
- value_weight: bfloat16 [2, 576, 192], P('section', 'fsdp'), may hold values from -0.25 to 0.25
- w_out: bfloat16 [2, 576, 576], P('section', None, 'fsdp'), may hold values from -4 to 4
- gain_mlp: bfloat16 [2, 576], P('section', 'fsdp'), may hold values from 0.5 to 1.5
- w_gate: bfloat16 [2, 576, 1536], P('section', 'fsdp'), may hold values from -0.25 to 0.25
- w_up: bfloat16 [2, 576, 1536], P('section', 'fsdp'), may hold values from -0.25 to 0.25
- w_down: bfloat16 [2, 1536, 576], P('section', None, 'fsdp'), may hold values from -0.15625 to 0.15625
Outputs:
- acts: bfloat16 [2, 4, 4, 1024, 576], P('section', None, 'fsdp', 'ctx')
- input_grads: bfloat16 [2, 4, 4, 1024, 576], P('section', None, 'fsdp', 'ctx')
- grad_gain_attn: float32 [2, 576], P('section', 'fsdp')
- grad_query: float32 [2, 576, 576], P('section', 'fsdp')
- grad_key: float32 [2, 576, 192], P('section', 'fsdp')
- grad_value: float32 [2, 576, 192], P('section', 'fsdp')
- grad_out: float32 [2, 576, 576], P('section', None, 'fsdp')
- grad_gain_mlp: float32 [2, 576], P('section', 'fsdp')
- grad_gate: float32 [2, 576, 1536], P('section', 'fsdp')
- grad_up: float32 [2, 576, 1536], P('section', 'fsdp')
- grad_down: float32 [2, 1536, 576], P('section', None, 'fsdp')
Inputs may be any that keep to these rules, and one draw needn't show every extreme that they name: `piece_order`: along the last dimension every number appears once, and entries 2c and 2c + 1 hold a pair j and 31 - j.
All inputs are finite; a program needn't handle non-finite values.
Results may differ from a plain program's by a relative error of at most 0.039.
Values may be sent and summed in bfloat16 or wider, within the bound.
A program may use at most 192 MiB of HBM per device.

v0:
```python
import math

import jax
import jax.numpy as jnp
from jax import lax
from jax.sharding import PartitionSpec as P

QUERY_HEADS = 9
KEY_VALUE_HEADS = 3
HEAD_SIZE = 64


eps_norm = 1e-05
rope_base = 100000.0
negative_filler = -1e30


def passed_along(block, axis, distance):
    devices = range(lax.axis_size(axis))
    route = [(i - distance, i) for i in devices if i - distance in devices]
    return lax.ppermute(block, axis, route)


def matrix_product(first_op, second_op):
    return jnp.dot(first_op, second_op, preferred_element_type=jnp.float32)


def times_trans(first_op, second_op):
    return lax.dot_general(
        first_op, second_op, (((1,), (1,)), ((), ())), preferred_element_type=jnp.float32
    )


def trans_times(first_op, second_op):
    return lax.dot_general(
        first_op, second_op, (((0,), (0,)), ((), ())), preferred_element_type=jnp.float32
    )


def rotary_embed(values, token_positions, turn_sign):
    half_dim = values.shape[-1] // 2
    frequency = rope_base ** (-jnp.arange(half_dim, dtype=jnp.float32) / half_dim)
    angles = token_positions.astype(jnp.float32)[:, None] * frequency[None, :]
    cosine = jnp.cos(angles)[:, None, :]
    sine_part = turn_sign * jnp.sin(angles)[:, None, :]
    first_half = values[..., :half_dim]
    second_half = values[..., half_dim:]
    return jnp.concatenate(
        [
            first_half * cosine - second_half * sine_part,
            second_half * cosine + first_half * sine_part,
        ],
        axis=-1,
    )


def normed(values, gain_vec):
    factor = lax.rsqrt(jnp.mean(values * values, axis=-1, keepdims=True) + eps_norm)
    return (values * factor * gain_vec, factor)


def normed_back(values, gain_vec, factor, upstream):
    scaled = upstream * gain_vec
    inner_mean = jnp.mean(scaled * values, axis=-1, keepdims=True)
    grad_values = factor * scaled - values * (factor * factor * factor) * inner_mean
    grad_gain = jnp.sum(upstream * values * factor, axis=0)
    return (grad_values, grad_gain)


def key_step(query_rows, local_position, whole_pos, state_now, key_pair):
    key_row_block, value_row_block = key_pair
    key_total_count = key_row_block.shape[0]
    key_head_rows = key_row_block.reshape(key_total_count, KEY_VALUE_HEADS, HEAD_SIZE)
    value_head_rows = value_row_block.reshape(key_total_count, KEY_VALUE_HEADS, HEAD_SIZE)
    allowed = (whole_pos[None, :] <= local_position[:, None])[:, None, None, :]
    scores = jnp.einsum(
        "qkgd,skd->qkgs", query_rows, key_head_rows, preferred_element_type=jnp.float32
    ) * (1.0 / math.sqrt(HEAD_SIZE))
    scores = jnp.where(allowed, scores, negative_filler)
    running, denominator, weighted = state_now
    highest = jnp.maximum(running, jnp.max(scores, axis=-1))
    weights_now = jnp.where(allowed, jnp.exp(scores - highest[..., None]), 0.0)
    denominator = jnp.sum(weights_now, axis=-1)
    weighted = jnp.einsum(
        "qkgs,skd->qkgd",
        weights_now.astype(jnp.bfloat16),
        value_head_rows,
        preferred_element_type=jnp.float32,
    )
    return (highest, denominator, weighted)


def key_grads(
    query_rows,
    grad_att,
    row_delta,
    log_total,
    local_position,
    whole_pos,
    key_row_block,
    value_row_block,
):
    key_total_count = key_row_block.shape[0]
    key_head_rows = key_row_block.reshape(key_total_count, KEY_VALUE_HEADS, HEAD_SIZE)
    value_head_rows = value_row_block.reshape(key_total_count, KEY_VALUE_HEADS, HEAD_SIZE)
    score_scale = 1.0 / math.sqrt(HEAD_SIZE)
    allowed = (whole_pos[None, :] <= local_position[:, None])[:, None, None, :]
    scores = (
        jnp.einsum("qkgd,skd->qkgs", query_rows, key_head_rows, preferred_element_type=jnp.float32)
        * score_scale
    )
    probs = jnp.where(allowed, jnp.exp(scores - log_total[..., None]), 0.0)
    grad_probs = jnp.einsum(
        "qkgd,skd->qkgs", grad_att, value_head_rows, preferred_element_type=jnp.float32
    )
    grad_scores = (probs * (grad_probs - row_delta[..., None])).astype(jnp.bfloat16)
    grad_queries = (
        jnp.einsum("qkgs,skd->qkgd", grad_scores, key_head_rows, preferred_element_type=jnp.float32)
        * score_scale
    )
    key_partial_terms = (
        jnp.einsum("qkgs,qkgd->skd", grad_scores, query_rows, preferred_element_type=jnp.float32)
        * score_scale
    )
    value_partial_terms = jnp.einsum(
        "qkgs,qkgd->skd", probs.astype(jnp.bfloat16), grad_att, preferred_element_type=jnp.float32
    )
    return (
        grad_queries,
        key_partial_terms.reshape(key_total_count, KEY_VALUE_HEADS * HEAD_SIZE),
        value_partial_terms.reshape(key_total_count, KEY_VALUE_HEADS * HEAD_SIZE),
    )


def body(
    inputs,
    piece_order,
    cotangent,
    gain_attn,
    w_query,
    key_weight,
    value_weight,
    w_out,
    gain_mlp,
    w_gate,
    w_up,
    w_down,
):
    section_index = lax.axis_index("section")
    ctx_index = lax.axis_index("ctx")
    ctx_count = lax.axis_size("ctx")
    micro_count = inputs.shape[0]
    row_total_count = inputs.shape[2]
    model_width = inputs.shape[3]
    piece_len = row_total_count // 2
    seq_length = row_total_count * ctx_count
    group_count = QUERY_HEADS // KEY_VALUE_HEADS
    gathered = (
        lax.all_gather(gain_attn[0], "fsdp", axis=0, tiled=True),
        lax.all_gather(w_query[0], "fsdp", axis=0, tiled=True),
        lax.all_gather(key_weight[0], "fsdp", axis=0, tiled=True),
        lax.all_gather(value_weight[0], "fsdp", axis=0, tiled=True),
        lax.all_gather(w_out[0], "fsdp", axis=1, tiled=True),
        lax.all_gather(gain_mlp[0], "fsdp", axis=0, tiled=True),
        lax.all_gather(w_gate[0], "fsdp", axis=0, tiled=True),
        lax.all_gather(w_up[0], "fsdp", axis=0, tiled=True),
        lax.all_gather(w_down[0], "fsdp", axis=1, tiled=True),
    )
    (
        gain_one,
        query_proj,
        key_projection,
        value_projection,
        out_proj,
        gain_two,
        gate_proj,
        up_proj,
        down_proj,
    ) = gathered
    gain_first = gain_one.astype(jnp.float32)
    gain_second = gain_two.astype(jnp.float32)

    def positions_at(slot):
        order_row = lax.dynamic_index_in_dim(piece_order[:, 0], slot, 0, keepdims=False)
        whole_pos = (
            order_row[:, None] * piece_len + jnp.arange(piece_len, dtype=jnp.int32)[None, :]
        ).reshape(seq_length)
        local_position = lax.dynamic_slice_in_dim(
            whole_pos, ctx_index * row_total_count, row_total_count
        )
        return (whole_pos, local_position)

    arriving = jnp.zeros((row_total_count, model_width), jnp.bfloat16)
    outputs_low = jnp.zeros((micro_count, row_total_count, model_width), jnp.bfloat16)
    stash_list = []
    for moment in range(micro_count + 1):
        micro_slot = moment - section_index
        active = (micro_slot >= 0) & (micro_slot < micro_count)
        clamped = jnp.clip(micro_slot, 0, micro_count - 1)
        whole_pos, local_position = positions_at(clamped)
        own_rows = lax.dynamic_index_in_dim(inputs[:, 0], clamped, 0, keepdims=False)
        layer_in = jnp.where(section_index == 0, own_rows, arriving)
        layer_start_val = layer_in.astype(jnp.float32)
        normed_one, layer_factor_one = normed(layer_start_val, gain_first)
        layer_normed_low = normed_one.astype(jnp.bfloat16)
        layer_query_rows = rotary_embed(
            matrix_product(layer_normed_low, query_proj).reshape(
                row_total_count, QUERY_HEADS, HEAD_SIZE
            ),
            local_position,
            1.0,
        )
        layer_query_rows = layer_query_rows.astype(jnp.bfloat16).reshape(
            row_total_count, KEY_VALUE_HEADS, group_count, HEAD_SIZE
        )
        key_row_block = rotary_embed(
            matrix_product(layer_normed_low, key_projection).reshape(
                row_total_count, KEY_VALUE_HEADS, HEAD_SIZE
            ),
            local_position,
            1.0,
        )
        key_row_block = key_row_block.astype(jnp.bfloat16).reshape(
            row_total_count, KEY_VALUE_HEADS * HEAD_SIZE
        )
        value_row_block = matrix_product(layer_normed_low, value_projection).astype(jnp.bfloat16)
        start_state = (
            jnp.full((row_total_count, KEY_VALUE_HEADS, group_count), negative_filler, jnp.float32),
            jnp.zeros((row_total_count, KEY_VALUE_HEADS, group_count), jnp.float32),
            jnp.zeros((row_total_count, KEY_VALUE_HEADS, group_count, HEAD_SIZE), jnp.float32),
        )
        running, denominator, weighted = key_step(
            layer_query_rows,
            local_position,
            whole_pos,
            start_state,
            (
                lax.all_gather(key_row_block, "ctx", axis=0, tiled=True),
                lax.all_gather(value_row_block, "ctx", axis=0, tiled=True),
            ),
        )
        layer_attended = weighted / denominator[..., None]
        layer_log_total = running + jnp.log(denominator)
        layer_att_low = layer_attended.reshape(row_total_count, QUERY_HEADS * HEAD_SIZE).astype(
            jnp.bfloat16
        )
        layer_hidden = layer_start_val + matrix_product(layer_att_low, out_proj)
        normed_two, layer_factor_two = normed(layer_hidden, gain_second)
        layer_normed_mid = normed_two.astype(jnp.bfloat16)
        layer_gate_val = matrix_product(layer_normed_mid, gate_proj)
        layer_up_val = matrix_product(layer_normed_mid, up_proj)
        layer_inner_low = (layer_gate_val * jax.nn.sigmoid(layer_gate_val) * layer_up_val).astype(
            jnp.bfloat16
        )
        result = layer_hidden + matrix_product(layer_inner_low, down_proj)
        layer_stored = (
            layer_start_val,
            layer_factor_one,
            layer_normed_low,
            layer_query_rows,
            key_row_block,
            value_row_block,
            layer_attended,
            layer_log_total,
            layer_att_low,
            layer_hidden,
            layer_factor_two,
            layer_normed_mid,
            layer_gate_val,
            layer_up_val,
            layer_inner_low,
        )
        result, stored = (result, layer_stored)
        result_low = result.astype(jnp.bfloat16)
        outputs_low = jnp.where(
            active,
            lax.dynamic_update_index_in_dim(outputs_low, result_low, clamped, 0),
            outputs_low,
        )
        stash_list.append(stored)
        if moment < micro_count:
            arriving = passed_along(result_low, "section", 1)
    stacked = jax.tree.map(lambda *tensors: jnp.stack(tensors), *stash_list)
    returning = jnp.zeros((row_total_count, model_width), jnp.bfloat16)
    grads_low = jnp.zeros((micro_count, row_total_count, model_width), jnp.bfloat16)
    totals = None
    for moment in range(micro_count + 1):
        micro_slot = moment - 1 + section_index
        active = (micro_slot >= 0) & (micro_slot < micro_count)
        clamped = jnp.clip(micro_slot, 0, micro_count - 1)
        stash_slot = jnp.clip(moment - 1 + 2 * section_index, 0, micro_count)
        stored = jax.tree.map(
            lambda tensor: lax.dynamic_index_in_dim(tensor, stash_slot, 0, keepdims=False), stacked
        )
        whole_pos, local_position = positions_at(clamped)
        own_grad = lax.dynamic_index_in_dim(cotangent[:, 0], clamped, 0, keepdims=False)
        upstream = jnp.where(section_index == 1, own_grad, returning).astype(jnp.float32)
        (
            start_val,
            factor_one,
            normed_low,
            query_rows,
            kept_keys,
            kept_values,
            attended,
            log_total,
            att_low,
            hidden,
            factor_two,
            normed_mid,
            gate_val,
            up_val,
            inner_low,
        ) = stored
        all_keys = lax.all_gather(kept_keys, "ctx", axis=0, tiled=True)
        all_values = lax.all_gather(kept_values, "ctx", axis=0, tiled=True)
        upstream_low = upstream.astype(jnp.bfloat16)
        grad_down = trans_times(inner_low, upstream_low)
        grad_inner = times_trans(upstream_low, down_proj)
        sigmoid_val = jax.nn.sigmoid(gate_val)
        gate_low = (
            grad_inner * up_val * sigmoid_val * (1.0 + gate_val * (1.0 - sigmoid_val))
        ).astype(jnp.bfloat16)
        up_low = (grad_inner * gate_val * sigmoid_val).astype(jnp.bfloat16)
        grad_gate = trans_times(normed_mid, gate_low)
        grad_up = trans_times(normed_mid, up_low)
        grad_mid = times_trans(gate_low, gate_proj) + times_trans(up_low, up_proj)
        back_hidden, grad_gain_two = normed_back(hidden, gain_second, factor_two, grad_mid)
        grad_hidden = upstream + back_hidden
        hidden_low = grad_hidden.astype(jnp.bfloat16)
        grad_out = trans_times(att_low, hidden_low)
        grad_att = (
            times_trans(hidden_low, out_proj)
            .astype(jnp.bfloat16)
            .reshape(row_total_count, KEY_VALUE_HEADS, group_count, HEAD_SIZE)
        )
        row_delta = jnp.sum(grad_att.astype(jnp.float32) * attended, axis=-1)
        grad_queries, key_partial_terms, value_partial_terms = key_grads(
            query_rows,
            grad_att,
            row_delta,
            log_total,
            local_position,
            whole_pos,
            all_keys,
            all_values,
        )
        key_gradient_sums = lax.psum_scatter(
            key_partial_terms.astype(jnp.bfloat16), "ctx", scatter_dimension=0, tiled=True
        ).astype(jnp.float32)
        value_sums = lax.psum_scatter(
            value_partial_terms.astype(jnp.bfloat16), "ctx", scatter_dimension=0, tiled=True
        )
        query_low = (
            rotary_embed(
                grad_queries.reshape(row_total_count, QUERY_HEADS, HEAD_SIZE), local_position, -1.0
            )
            .reshape(row_total_count, QUERY_HEADS * HEAD_SIZE)
            .astype(jnp.bfloat16)
        )
        key_low = (
            rotary_embed(
                key_gradient_sums.reshape(row_total_count, KEY_VALUE_HEADS, HEAD_SIZE),
                local_position,
                -1.0,
            )
            .reshape(row_total_count, KEY_VALUE_HEADS * HEAD_SIZE)
            .astype(jnp.bfloat16)
        )
        grad_query = trans_times(normed_low, query_low)
        grad_key = trans_times(normed_low, key_low)
        grad_value = trans_times(normed_low, value_sums)
        grad_normed = (
            times_trans(query_low, query_proj)
            + times_trans(key_low, key_projection)
            + times_trans(value_sums, value_projection)
        )
        back_start, grad_gain_one = normed_back(start_val, gain_first, factor_one, grad_normed)
        grad_input = grad_hidden + back_start
        terms = (
            grad_gain_one,
            grad_query,
            grad_key,
            grad_value,
            grad_out,
            grad_gain_two,
            grad_gate,
            grad_up,
            grad_down,
        )
        grad_input_low = grad_input.astype(jnp.bfloat16)
        grads_low = jnp.where(
            active,
            lax.dynamic_update_index_in_dim(grads_low, grad_input_low, clamped, 0),
            grads_low,
        )
        terms = jax.tree.map(lambda tensor: jnp.where(active, tensor, 0.0), terms)
        totals = (
            terms
            if totals is None
            else jax.tree.map(lambda before, after: before + after, totals, terms)
        )
        if moment < micro_count:
            returning = passed_along(grad_input_low, "section", -1)
    (
        total_gain_attn,
        total_query,
        total_key,
        total_value,
        total_out,
        total_gain_mlp,
        total_gate,
        total_up,
        total_down,
    ) = totals
    shares = (
        lax.psum_scatter(
            total_gain_attn.astype(jnp.bfloat16), "fsdp", scatter_dimension=0, tiled=True
        ).astype(jnp.float32),
        lax.psum_scatter(
            total_query.astype(jnp.bfloat16), "fsdp", scatter_dimension=0, tiled=True
        ).astype(jnp.float32),
        lax.psum_scatter(
            total_key.astype(jnp.bfloat16), "fsdp", scatter_dimension=0, tiled=True
        ).astype(jnp.float32),
        lax.psum_scatter(
            total_value.astype(jnp.bfloat16), "fsdp", scatter_dimension=0, tiled=True
        ).astype(jnp.float32),
        lax.psum_scatter(
            total_out.astype(jnp.bfloat16), "fsdp", scatter_dimension=1, tiled=True
        ).astype(jnp.float32),
        lax.psum_scatter(
            total_gain_mlp.astype(jnp.bfloat16), "fsdp", scatter_dimension=0, tiled=True
        ).astype(jnp.float32),
        lax.psum_scatter(
            total_gate.astype(jnp.bfloat16), "fsdp", scatter_dimension=0, tiled=True
        ).astype(jnp.float32),
        lax.psum_scatter(
            total_up.astype(jnp.bfloat16), "fsdp", scatter_dimension=0, tiled=True
        ).astype(jnp.float32),
        lax.psum_scatter(
            total_down.astype(jnp.bfloat16), "fsdp", scatter_dimension=1, tiled=True
        ).astype(jnp.float32),
    )
    summed = (
        lax.psum(shares[0].astype(jnp.bfloat16), "ctx").astype(jnp.float32),
        lax.psum(shares[1].astype(jnp.bfloat16), "ctx").astype(jnp.float32),
        lax.psum(shares[2].astype(jnp.bfloat16), "ctx").astype(jnp.float32),
        lax.psum(shares[3].astype(jnp.bfloat16), "ctx").astype(jnp.float32),
        lax.psum(shares[4].astype(jnp.bfloat16), "ctx").astype(jnp.float32),
        lax.psum(shares[5].astype(jnp.bfloat16), "ctx").astype(jnp.float32),
        lax.psum(shares[6].astype(jnp.bfloat16), "ctx").astype(jnp.float32),
        lax.psum(shares[7].astype(jnp.bfloat16), "ctx").astype(jnp.float32),
        lax.psum(shares[8].astype(jnp.bfloat16), "ctx").astype(jnp.float32),
    )
    return (
        outputs_low[None, :, None],
        grads_low[None, :, None],
        summed[0][None],
        summed[1][None],
        summed[2][None],
        summed[3][None],
        summed[4][None],
        summed[5][None],
        summed[6][None],
        summed[7][None],
        summed[8][None],
    )


def solution(mesh):
    placed = (
        P(None, "fsdp", "ctx", None),
        P(None, "fsdp", None),
        P(None, "fsdp", "ctx", None),
        P("section", "fsdp"),
        P("section", "fsdp", None),
        P("section", "fsdp", None),
        P("section", "fsdp", None),
        P("section", None, "fsdp"),
        P("section", "fsdp"),
        P("section", "fsdp", None),
        P("section", "fsdp", None),
        P("section", None, "fsdp"),
    )
    return jax.shard_map(
        body,
        mesh=mesh,
        in_specs=placed,
        out_specs=(
            P("section", None, "fsdp", "ctx", None),
            P("section", None, "fsdp", "ctx", None),
            P("section", "fsdp"),
            P("section", "fsdp", None),
            P("section", "fsdp", None),
            P("section", "fsdp", None),
            P("section", None, "fsdp"),
            P("section", "fsdp"),
            P("section", "fsdp", None),
            P("section", "fsdp", None),
            P("section", None, "fsdp"),
        ),
        check_vma=False,
    )
```

profile of v0, /device:TPU:0, one launch (start us, length us, event | category | flops | bytes accessed | tf_op | source)
XLA Modules:
  0.0 2013.2 jit_solution(8516633762930319999)
XLA Ops:
  13.3 14.2 all-gather.2
  29.5 11.7 all-reduce.7
  49.4 24.2 %all_gather.91 = bf16[1024,192]{1,0:T(8,128)(2,1)S(1)} all-gather(bf16[64,192]{1,0:T(8,128)(2,1)S(1)} %copy.174), channel_id=1, replica_groups=mesh['section'=2,'ctx'=16,'fsdp'=4] {'ctx'}, dimensions={0}, use_global_device_ids=true | all-gather | bytes 417792 | tf_op jit(solution)/shard_map/all_gather | solution.py:238
  74.6 15.3 all-gather.3
  93.1 13.2 all-gather.1
  108.1 23.0 %all_gather.89 = bf16[1024,192]{1,0:T(8,128)(2,1)S(1)} all-gather(bf16[64,192]{1,0:T(8,128)(2,1)S(1)} %get-tuple-element.340), channel_id=1, replica_groups=mesh['section'=2,'ctx'=16,'fsdp'=4] {'ctx'}, dimensions={0}, use_global_device_ids=true | all-gather | bytes 417792 | tf_op jit(solution)/shard_map/all_gather | solution.py:239
  132.1 13.5 all-gather.4
  174.8 2.8 bitcast_dynamic-update-slice_fusion.4
  177.6 2.9 bitcast_dynamic-update-slice_fusion.19
  187.8 24.2 %all_gather.99 = bf16[1024,192]{1,0:T(8,128)(2,1)} all-gather(bf16[64,192]{1,0:T(8,128)(2,1)S(1)} %copy.181), channel_id=1, replica_groups=mesh['section'=2,'ctx'=16,'fsdp'=4] {'ctx'}, dimensions={0}, use_global_device_ids=true | all-gather | bytes 417792 | tf_op jit(solution)/shard_map/all_gather | solution.py:238
  216.7 3.1 fusion.21
  221.4 23.1 %all_gather.98 = bf16[1024,192]{1,0:T(8,128)(2,1)S(1)} all-gather(bf16[64,192]{1,0:T(8,128)(2,1)S(1)} %get-tuple-element.342), channel_id=1, replica_groups=mesh['section'=2,'ctx'=16,'fsdp'=4] {'ctx'}, dimensions={0}, use_global_device_ids=true | all-gather | bytes 417792 | tf_op jit(solution)/shard_map/all_gather | solution.py:239
  248.0 2.7 fusion.766
  279.0 24.2 %all_gather.101 = bf16[1024,192]{1,0:T(8,128)(2,1)} all-gather(bf16[64,192]{1,0:T(8,128)(2,1)} %copy.188), channel_id=1, replica_groups=mesh['section'=2,'ctx'=16,'fsdp'=4] {'ctx'}, dimensions={0}, use_global_device_ids=true | all-gather | bytes 417792 | tf_op jit(solution)/shard_map/all_gather | solution.py:238
  310.2 3.2 fusion.22
  315.5 24.6 %all_gather.100 = bf16[1024,192]{1,0:T(8,128)(2,1)} all-gather(bf16[64,192]{1,0:T(8,128)(2,1)S(1)} %get-tuple-element.344), channel_id=1, replica_groups=mesh['section'=2,'ctx'=16,'fsdp'=4] {'ctx'}, dimensions={0}, use_global_device_ids=true | all-gather | bytes 417792 | tf_op jit(solution)/shard_map/all_gather | solution.py:239
  375.4 24.2 %all_gather.103 = bf16[1024,192]{1,0:T(8,128)(2,1)} all-gather(bf16[64,192]{1,0:T(8,128)(2,1)} %copy.195), channel_id=1, replica_groups=mesh['section'=2,'ctx'=16,'fsdp'=4] {'ctx'}, dimensions={0}, use_global_device_ids=true | all-gather | bytes 417792 | tf_op jit(solution)/shard_map/all_gather | solution.py:238
  406.7 3.2 fusion.23
  412.0 25.0 %all_gather.102 = bf16[1024,192]{1,0:T(8,128)(2,1)} all-gather(bf16[64,192]{1,0:T(8,128)(2,1)S(1)} %get-tuple-element.346), channel_id=1, replica_groups=mesh['section'=2,'ctx'=16,'fsdp'=4] {'ctx'}, dimensions={0}, use_global_device_ids=true | all-gather | bytes 417792 | tf_op jit(solution)/shard_map/all_gather | solution.py:239
  472.1 24.2 %all_gather.105 = bf16[1024,192]{1,0:T(8,128)(2,1)} all-gather(bf16[64,192]{1,0:T(8,128)(2,1)} %copy.202), channel_id=1, replica_groups=mesh['section'=2,'ctx'=16,'fsdp'=4] {'ctx'}, dimensions={0}, use_global_device_ids=true | all-gather | bytes 417792 | tf_op jit(solution)/shard_map/all_gather | solution.py:238
  503.4 3.2 fusion.24
  508.6 24.6 %all_gather.104 = bf16[1024,192]{1,0:T(8,128)(2,1)} all-gather(bf16[64,192]{1,0:T(8,128)(2,1)S(1)} %get-tuple-element.348), channel_id=1, replica_groups=mesh['section'=2,'ctx'=16,'fsdp'=4] {'ctx'}, dimensions={0}, use_global_device_ids=true | all-gather | bytes 417792 | tf_op jit(solution)/shard_map/all_gather | solution.py:239
  562.4 24.5 %all-gather.9 = bf16[1,1024,192]{2,1,0:T(8,128)(2,1)} all-gather(bf16[1,64,192]{2,1,0:T(8,128)(2,1)S(1)} %get-tuple-element.192), channel_id=11, replica_groups=mesh['section'=2,'ctx'=16,'fsdp'=4] {'ctx'}, dimensions={1}, use_global_device_ids=true | all-gather | bytes 417792 | tf_op jit(solution)/shard_map/all_gather | solution.py:315
  601.1 24.6 %all-gather.10 = bf16[1,1024,192]{2,1,0:T(8,128)(2,1)} all-gather(bf16[1,64,192]{2,1,0:T(8,128)(2,1)S(1)} %get-tuple-element.187), channel_id=12, replica_groups=mesh['section'=2,'ctx'=16,'fsdp'=4] {'ctx'}, dimensions={1}, use_global_device_ids=true | all-gather | bytes 417792 | tf_op jit(solution)/shard_map/all_gather | solution.py:316
  630.4 2.8 fusion.17
  638.4 24.5 %all-gather.11 = bf16[1,1024,192]{2,1,0:T(8,128)(2,1)} all-gather(bf16[1,64,192]{2,1,0:T(8,128)(2,1)} %get-tuple-element.191), channel_id=13, replica_groups=mesh['section'=2,'ctx'=16,'fsdp'=4] {'ctx'}, dimensions={1}, use_global_device_ids=true | all-gather | bytes 417792 | tf_op jit(solution)/shard_map/all_gather | solution.py:315
  664.9 3.0 fusion.495
  667.9 24.6 %all-gather.12 = bf16[1,1024,192]{2,1,0:T(8,128)(2,1)} all-gather(bf16[1,64,192]{2,1,0:T(8,128)(2,1)S(1)} %copy-done.161), channel_id=14, replica_groups=mesh['section'=2,'ctx'=16,'fsdp'=4] {'ctx'}, dimensions={1}, use_global_device_ids=true | all-gather | bytes 417792 | tf_op jit(solution)/shard_map/all_gather | solution.py:316
  694.6 24.6 %all-gather.13 = bf16[1,1024,192]{2,1,0:T(8,128)(2,1)} all-gather(bf16[1,64,192]{2,1,0:T(8,128)(2,1)} %get-tuple-element.190), channel_id=15, replica_groups=mesh['section'=2,'ctx'=16,'fsdp'=4] {'ctx'}, dimensions={1}, use_global_device_ids=true | all-gather | bytes 417792 | tf_op jit(solution)/shard_map/all_gather | solution.py:315
  721.2 3.1 fusion.492
  724.3 24.6 %all-gather.14 = bf16[1,1024,192]{2,1,0:T(8,128)(2,1)} all-gather(bf16[1,64,192]{2,1,0:T(8,128)(2,1)S(1)} %copy-done.160), channel_id=16, replica_groups=mesh['section'=2,'ctx'=16,'fsdp'=4] {'ctx'}, dimensions={1}, use_global_device_ids=true | all-gather | bytes 417792 | tf_op jit(solution)/shard_map/all_gather | solution.py:316
  750.8 24.3 %all-gather.15 = bf16[1,1024,192]{2,1,0:T(8,128)(2,1)} all-gather(bf16[1,64,192]{2,1,0:T(8,128)(2,1)} %get-tuple-element.189), channel_id=17, replica_groups=mesh['section'=2,'ctx'=16,'fsdp'=4] {'ctx'}, dimensions={1}, use_global_device_ids=true | all-gather | bytes 417792 | tf_op jit(solution)/shard_map/all_gather | solution.py:315
  777.1 24.5 %all-gather.16 = bf16[1,1024,192]{2,1,0:T(8,128)(2,1)} all-gather(bf16[1,64,192]{2,1,0:T(8,128)(2,1)} %get-tuple-element.184), channel_id=18, replica_groups=mesh['section'=2,'ctx'=16,'fsdp'=4] {'ctx'}, dimensions={1}, use_global_device_ids=true | all-gather | bytes 417792 | tf_op jit(solution)/shard_map/all_gather | solution.py:316
  803.6 24.3 %all-gather.17 = bf16[1,1024,192]{2,1,0:T(8,128)(2,1)} all-gather(bf16[1,64,192]{2,1,0:T(8,128)(2,1)} %get-tuple-element.188), channel_id=19, replica_groups=mesh['section'=2,'ctx'=16,'fsdp'=4] {'ctx'}, dimensions={1}, use_global_device_ids=true | all-gather | bytes 417792 | tf_op jit(solution)/shard_map/all_gather | solution.py:315
  829.9 24.5 %all-gather.18 = bf16[1,1024,192]{2,1,0:T(8,128)(2,1)} all-gather(bf16[1,64,192]{2,1,0:T(8,128)(2,1)} %get-tuple-element.183), channel_id=20, replica_groups=mesh['section'=2,'ctx'=16,'fsdp'=4] {'ctx'}, dimensions={1}, use_global_device_ids=true | all-gather | bytes 417792 | tf_op jit(solution)/shard_map/all_gather | solution.py:316
  856.4 2.7 convolution_multiply_fusion.4
  859.1 2.9 fusion.489
  862.0 2.9 fusion.486
  875.3 58.6 %reduce-scatter.54.cloned.1.call-done = bf16[64,192]{1,0:T(8,128)(2,1)} async-done(((bf16[1024,192]{1,0:T(8,128)(2,1)}), bf16[64,192]{1,0:T(8,128)(2,1)}) %reduce-scatter.54.cloned.1.call-update) | async-done | bytes 24592
  955.0 2.8 fusion.13
  965.0 3.1 fusion.115
  970.1 2.7 convolution_multiply_fusion.3
  972.9 3.5 convolution_select_fusion.13
  977.1 58.3 %reduce-scatter.56.cloned.1.call-done = bf16[64,192]{1,0:T(8,128)(2,1)} async-done(((bf16[1024,192]{1,0:T(8,128)(2,1)}), bf16[64,192]{1,0:T(8,128)(2,1)}) %reduce-scatter.56.cloned.1.call-update) | async-done | bytes 24592
  1040.0 70.6 %reduce-scatter.58.cloned.1.call-done = bf16[64,192]{1,0:T(8,128)(2,1)} async-done(((bf16[1024,192]{1,0:T(8,128)(2,1)}), bf16[64,192]{1,0:T(8,128)(2,1)}) %reduce-scatter.58.cloned.1.call-update) | async-done | bytes 24592
  1130.4 2.8 fusion.9
  1140.9 3.1 fusion.116
  1150.5 60.4 %reduce-scatter.60.cloned.1.call-done = bf16[64,192]{1,0:T(8,128)(2,1)} async-done(((bf16[1024,192]{1,0:T(8,128)(2,1)}), bf16[64,192]{1,0:T(8,128)(2,1)}) %reduce-scatter.60.cloned.1.call-update) | async-done | bytes 24592
  1215.4 70.5 %reduce-scatter.62.cloned.1.call-done = bf16[64,192]{1,0:T(8,128)(2,1)} async-done(((bf16[1024,192]{1,0:T(8,128)(2,1)}), bf16[64,192]{1,0:T(8,128)(2,1)}) %reduce-scatter.62.cloned.1.call-update) | async-done | bytes 24592
  1305.8 2.8 fusion.5
  1316.0 3.1 fusion.117
  1325.6 60.6 %reduce-scatter.64.cloned.1.call-done = bf16[64,192]{1,0:T(8,128)(2,1)} async-done(((bf16[1024,192]{1,0:T(8,128)(2,1)}), bf16[64,192]{1,0:T(8,128)(2,1)}) %reduce-scatter.64.cloned.1.call-update) | async-done | bytes 24592
  1390.7 70.5 %reduce-scatter.66.cloned.1.call-done = bf16[64,192]{1,0:T(8,128)(2,1)} async-done(((bf16[1024,192]{1,0:T(8,128)(2,1)}), bf16[64,192]{1,0:T(8,128)(2,1)}) %reduce-scatter.66.cloned.1.call-update) | async-done | bytes 24592
  1488.3 68.4 %reduce-scatter.68.cloned.1.call-done = bf16[64,192]{1,0:T(8,128)(2,1)} async-done(((bf16[1024,192]{1,0:T(8,128)(2,1)}), bf16[64,192]{1,0:T(8,128)(2,1)}) %reduce-scatter.68.cloned.1.call-update) | async-done | bytes 24592
  1561.0 71.3 %reduce-scatter.70.cloned.1.call-done = bf16[64,192]{1,0:T(8,128)(2,1)} async-done(((bf16[1024,192]{1,0:T(8,128)(2,1)}), bf16[64,192]{1,0:T(8,128)(2,1)}) %reduce-scatter.70.cloned.1.call-update) | async-done | bytes 24592
  1635.9 3.0 add_convert_fusion.3
  1667.8 10.8 all-reduce.6
  1680.0 23.3 %reduce-scatter.72.cloned.1.call-done = bf16[144,576]{1,0:T(8,128)(2,1)} async-done(((bf16[576,576]{1,0:T(8,128)(2,1)}), bf16[144,576]{1,0:T(8,128)(2,1)}) %reduce-scatter.72.cloned.1.call-update) | async-done | bytes 165904
  1705.2 23.1 %reduce-scatter.40.cloned.1.call-done = bf16[144,576]{1,0:T(8,128)(2,1)} async-done(((bf16[576,576]{1,0:T(8,128)(2,1)}), bf16[144,576]{1,0:T(8,128)(2,1)}) %reduce-scatter.40.cloned.1.call-update) | async-done | bytes 165904 | tf_op jit(solution)/shard_map/reduce_scatter | solution.py:420
  1728.3 29.1 %reduce-scatter.46.cloned.1.call-done = bf16[144,1536]{1,0:T(8,128)(2,1)} async-done(((bf16[576,1536]{1,0:T(8,128)(2,1)}), bf16[144,1536]{1,0:T(8,128)(2,1)}) %reduce-scatter.46.cloned.1.call-update) | async-done | bytes 442384 | tf_op jit(solution)/shard_map/reduce_scatter | solution.py:435
  1757.4 29.4 %reduce-scatter.48.cloned.1.call-done = bf16[144,1536]{1,0:T(8,128)(2,1)} async-done(((bf16[576,1536]{1,0:T(8,128)(2,1)}), bf16[144,1536]{1,0:T(8,128)(2,1)}) %reduce-scatter.48.cloned.1.call-update) | async-done | bytes 442384 | tf_op jit(solution)/shard_map/reduce_scatter | solution.py:438
  1786.8 29.1 %reduce-scatter.50.cloned.1.call-done = bf16[1536,144]{0,1:T(8,128)(2,1)} async-done(((bf16[1536,576]{0,1:T(8,128)(2,1)}), bf16[1536,144]{0,1:T(8,128)(2,1)}) %reduce-scatter.50.cloned.1.call-update) | async-done | bytes 442384 | tf_op jit(solution)/shard_map/reduce_scatter | solution.py:441
  1818.0 85.9 %all-reduce.11.cloned.1.call-done = (bf16[1,144]{1,0:T(2,128)(2,1)}, bf16[1,144,192]{2,1,0:T(8,128)(2,1)}, bf16[1,144,192]{2,1,0:T(8,128)(2,1)}, bf16[1,144]{1,0:T(2,128)(2,1)}) async-done(((bf16[1,144]{1,0:T(2,128)(2,1)}, bf16[1,144,192]{2,1,0:T(8,128)(2,1)}, bf16[1,144,192]{2,1,0:T(8,128)(2,1)}, bf16[1,144]{1,0:T(2,128)(2,1)}), (bf16[1,144]{1,0:T(2,128)(2,1)}, bf16[1,144,192]{2,1,0:T(8,128)(2,1)}, ...) | async-done | bytes 111184 | tf_op jit(solution)/shard_map/psum | solution.py:446
  1909.5 89.1 %all-reduce.13.cloned.1.call-done = (bf16[1,576,144]{2,1,0:T(8,128)(2,1)}, bf16[1,144,576]{2,1,0:T(8,128)(2,1)}, bf16[1,144,1536]{2,1,0:T(8,128)(2,1)}, bf16[1,1...) async-done(((bf16[1,576,144]{2,1,0:T(8,128)(2,1)}, bf16[1,144,576]{2,1,0:T(8,128)(2,1)}, bf16[1,144,1536]{2,1,0:T(8,128)(2,1)}, bf16[1,144,1536]{2,1,0:T(8,128)(2,1)}, ...) | async-done | bytes 1658896 | tf_op jit(solution)/shard_map/psum | solution.py:450
  (934 shorter events, 466.2 us)
Async XLA Ops:
  7.2 20.6 %copy-start.217 = (u32[128]{0:T(128)S(1)}, u32[128]{0:T(128)}, u32[]{:S(2)}) copy-start(u32[128]{0:T(128)} %constant.362) | copy-start | bytes 1540
  7.2 40.5 %copy-start.77 = (bf16[4,1,64,576]{3,2,1,0:T(8,128)(2,1)S(1)}, bf16[4,1,64,576]{3,2,1,0:T(8,128)(2,1)}, u32[]{:S(2)}) copy-start(bf16[4,1,64,576]{3,2,1,0:T(8,128)(2,1)} %param.12) | copy-start | bytes 884740
  7.2 20.5 %copy-start.219 = (bf16[1,144]{1,0:T(2,128)(2,1)S(1)}, bf16[1,144]{1,0:T(2,128)(2,1)}, u32[]{:S(2)}) copy-start(bf16[1,144]{1,0:T(2,128)(2,1)} %param.15) | copy-start | bytes 868
  7.2 20.5 %copy-start.220 = (bf16[1,144]{1,0:T(2,128)(2,1)S(1)}, bf16[1,144]{1,0:T(2,128)(2,1)}, u32[]{:S(2)}) copy-start(bf16[1,144]{1,0:T(2,128)(2,1)} %param.20) | copy-start | bytes 868
  7.2 167.6 %all-gather.23.cloned.1.call-start = ((), (), s32[]{:S(2)}) async-start(), calls=%async_computation.23 | async-start | bytes 2211840 | tf_op jit(solution)/shard_map/all_gather | solution.py:165
  8.0 169.7 %all-gather.25.cloned.1.call-start = ((), (), s32[]{:S(2)}) async-start(), calls=%async_computation.24 | async-start | bytes 2211840 | tf_op jit(solution)/shard_map/all_gather | solution.py:166
  8.7 171.8 %all-gather.27.cloned.1.call-start = ((), (), s32[]{:S(2)}) async-start(), calls=%async_computation.25 | async-start | bytes 2211840 | tf_op jit(solution)/shard_map/all_gather | solution.py:167
  9.4 65.1 %copy-start.146 = (bf16[1,144,576]{2,1,0:T(8,128)(2,1)S(1)}, bf16[1,144,576]{2,1,0:T(8,128)(2,1)}, u32[]{:S(2)}) copy-start(bf16[1,144,576]{2,1,0:T(8,128)(2,1)} %param.16) | copy-start | bytes 497668
  9.5 861.3 %reduce-scatter.52.cloned.1.call-start = ((), (), s32[]{:S(2)}) async-start(), calls=%async_computation.26 | async-start | bytes 557056
  10.6 37.1 %copy-start.221 = (f32[64]{0:T(128)}, f32[64]{0:T(128)S(1)}, u32[]{:S(2)}) copy-start(f32[64]{0:T(128)S(1)} %fusion.379) | copy-start | bytes 772
  41.2 49.1 %copy-start.207 = (f32[64]{0:T(128)}, f32[64]{0:T(128)S(1)}, u32[]{:S(2)}) copy-start(f32[64]{0:T(128)S(1)} %add_rsqrt_fusion.9) | copy-start | bytes 772
  45.6 44.6 %copy-start.175 = (s32[1024]{0:T(1024)}, s32[1024]{0:T(1024)S(1)}, u32[]{:S(2)}) copy-start(s32[1024]{0:T(1024)S(1)} %add.1050) | copy-start | bytes 12292
  49.3 40.9 %copy-start.136 = (bf16[64,3,64]{0,2,1:T(8,128)(2,1)}, bf16[64,3,64]{0,2,1:T(8,128)(2,1)S(1)}, u32[]{:S(2)}) copy-start(bf16[64,3,64]{0,2,1:T(8,128)(2,1)S(1)} %maximum_convert_fusion.5) | copy-start | bytes 73732
  74.6 16.5 copy-start.79
  74.6 16.5 copy-start.123
  90.8 17.3 copy-start.115
  106.3 113.5 %copy-start.18 = (bf16[1,576,192]{2,1,0:T(8,128)(2,1)}, bf16[1,576,192]{2,1,0:T(8,128)(2,1)S(1)}, u32[]{:S(2)}) copy-start(bf16[1,576,192]{2,1,0:T(8,128)(2,1)S(1)} %all-gather.1) | copy-start | bytes 663556
  132.1 16.0 copy-start.141
  182.8 65.1 %copy-start.55 = (bf16[4,64,576]{2,1,0:T(8,128)(2,1)}, bf16[4,64,576]{2,1,0:T(8,128)(2,1)S(1)}, u32[]{:S(2)}) copy-start(bf16[4,64,576]{2,1,0:T(8,128)(2,1)S(1)} %get-tuple-element.292) | copy-start | bytes 884740
  182.9 2.2 collective-permute-start
  184.9 31.8 %copy-start.122 = (pred[64,1024]{1,0:T(8,128)(4,1)S(1)}, pred[64,1024]{1,0:T(8,128)(4,1)}, u32[]{:S(2)}) copy-start(pred[64,1024]{1,0:T(8,128)(4,1)} %broadcast_compare_fusion.8) | copy-start | bytes 196612
  186.0 33.9 %copy-start.52 = (f32[5,64,576]{2,1,0:T(8,128)}, f32[5,64,576]{2,1,0:T(8,128)S(1)}, u32[]{:S(2)}) copy-start(f32[5,64,576]{2,1,0:T(8,128)S(1)} %get-tuple-element.137) | copy-start | bytes 2211844
  186.0 33.9 %copy-start.44 = (bf16[64,576]{1,0:T(8,128)(2,1)}, bf16[64,576]{1,0:T(8,128)(2,1)S(1)}, u32[]{:S(2)}) copy-start(bf16[64,576]{1,0:T(8,128)(2,1)S(1)} %get-tuple-element.138) | copy-start | bytes 221188
  187.7 26.3 %copy-start.135 = (bf16[64,3,64]{0,2,1:T(8,128)(2,1)}, bf16[64,3,64]{0,2,1:T(8,128)(2,1)S(1)}, u32[]{:S(2)}) copy-start(bf16[64,3,64]{0,2,1:T(8,128)(2,1)S(1)} %maximum_convert_fusion.6) | copy-start | bytes 73732
  215.1 30.3 %copy-start.113 = (bf16[64,9,32]{0,2,1:T(8,128)(2,1)}, bf16[64,9,32]{0,2,1:T(8,128)(2,1)S(1)}, u32[]{:S(2)}) copy-start(bf16[64,9,32]{0,2,1:T(8,128)(2,1)S(1)} %get-tuple-element.179) | copy-start | bytes 110596
  215.1 30.3 %copy-start.114 = (bf16[64,9,32]{0,2,1:T(8,128)(2,1)}, bf16[64,9,32]{0,2,1:T(8,128)(2,1)S(1)}, u32[]{:S(2)}) copy-start(bf16[64,9,32]{0,2,1:T(8,128)(2,1)S(1)} %get-tuple-element.180) | copy-start | bytes 110596
  219.8 28.1 %copy-start.167 = (f32[64,3,3]{0,2,1:T(4,128)}, f32[64,3,3]{0,2,1:T(4,128)S(1)}, u32[]{:S(2)}) copy-start(f32[64,3,3]{0,2,1:T(4,128)S(1)} %broadcast_maximum_fusion.3) | copy-start | bytes 6916
  256.7 16.3 collective-permute-start.1
  353.2 16.2 collective-permute-start.2
  450.1 16.2 collective-permute-start.3
  638.4 295.6 %reduce-scatter.54.cloned.1.call-start = ((), (), s32[]{:S(2)}) async-start(), calls=%async_computation.27 | async-start | bytes 557056
  864.9 170.5 %reduce-scatter.56.cloned.1.call-start = ((), (), s32[]{:S(2)}) async-start(), calls=%async_computation.28 | async-start | bytes 557056
  868.3 68.6 %copy-start.199 = (f32[64]{0:T(128)S(1)}, f32[64]{0:T(128)}, u32[]{:S(2)}) copy-start(f32[64]{0:T(128)} %copy-done.198) | copy-start | bytes 772
  938.7 6.0 collective-permute-start.4
  963.0 147.6 %reduce-scatter.58.cloned.1.call-start = ((), (), s32[]{:S(2)}) async-start(), calls=%async_computation.29 | async-start | bytes 557056
  972.8 238.0 %reduce-scatter.60.cloned.1.call-start = ((), (), s32[]{:S(2)}) async-start(), calls=%async_computation.30 | async-start | bytes 557056
  1115.8 3.7 collective-permute-start.5
  1138.4 147.5 %reduce-scatter.62.cloned.1.call-start = ((), (), s32[]{:S(2)}) async-start(), calls=%async_computation.31 | async-start | bytes 557056
  1148.7 237.5 %reduce-scatter.64.cloned.1.call-start = ((), (), s32[]{:S(2)}) async-start(), calls=%async_computation.32 | async-start | bytes 557056
  1291.1 3.8 collective-permute-start.6
  1313.7 147.5 %reduce-scatter.66.cloned.1.call-start = ((), (), s32[]{:S(2)}) async-start(), calls=%async_computation.33 | async-start | bytes 557056
  1323.8 232.9 %reduce-scatter.68.cloned.1.call-start = ((), (), s32[]{:S(2)}) async-start(), calls=%async_computation.34 | async-start | bytes 557056
  1466.4 3.7 collective-permute-start.7
  1476.7 159.1 %copy-start.61 = (f32[64,576]{1,0:T(8,128)}, f32[64,576]{1,0:T(8,128)S(1)}, u32[]{:S(2)}) copy-start(f32[64,576]{1,0:T(8,128)S(1)} %fusion.409) | copy-start | bytes 442372
  1484.3 148.1 %reduce-scatter.70.cloned.1.call-start = ((), (), s32[]{:S(2)}) async-start(), calls=%async_computation.35 | async-start | bytes 557056
  1486.9 70.7 %copy-start.147 = (f32[64,32]{0,1:T(8,128)S(1)}, f32[64,32]{0,1:T(8,128)}, u32[]{:S(2)}) copy-start(f32[64,32]{0,1:T(8,128)} %get-tuple-element.245) | copy-start | bytes 24580
  1486.9 70.7 %copy-start.148 = (f32[64,32]{0,1:T(8,128)S(1)}, f32[64,32]{0,1:T(8,128)}, u32[]{:S(2)}) copy-start(f32[64,32]{0,1:T(8,128)} %get-tuple-element.246) | copy-start | bytes 24580
  1487.9 192.1 %reduce-scatter.42.cloned.1.call-start = ((), (), s32[]{:S(2)}) async-start(), calls=%async_computation.18 | async-start | bytes 368640 | tf_op jit(solution)/shard_map/reduce_scatter | solution.py:423
  1488.3 146.2 %copy-start.64 = (f32[64,576]{1,0:T(8,128)S(1)}, f32[64,576]{1,0:T(8,128)}, u32[]{:S(2)}) copy-start(f32[64,576]{1,0:T(8,128)} %copy-done.63) | copy-start | bytes 442372
  1558.6 77.2 %copy-start.29 = (f32[576,576]{1,0:T(8,128)S(1)}, f32[576,576]{1,0:T(8,128)}, u32[]{:S(2)}) copy-start(f32[576,576]{1,0:T(8,128)} %fusion.507) | copy-start | bytes 3981316
  1558.7 121.3 %reduce-scatter.44.cloned.1.call-start = ((), (), s32[]{:S(2)}) async-start(), calls=%async_computation.19 | async-start | bytes 368640 | tf_op jit(solution)/shard_map/reduce_scatter | solution.py:426
  1634.4 69.0 %reduce-scatter.72.cloned.1.call-start = ((), (), s32[]{:S(2)}) async-start(), calls=%async_computation.36 | async-start | bytes 921600
  1641.2 87.0 %reduce-scatter.40.cloned.1.call-start = ((), (), s32[]{:S(2)}) async-start(), calls=%async_computation.17 | async-start | bytes 921600 | tf_op jit(solution)/shard_map/reduce_scatter | solution.py:420
  1645.4 112.0 %reduce-scatter.46.cloned.1.call-start = ((), (), s32[]{:S(2)}) async-start(), calls=%async_computation.20 | async-start | bytes 2211840 | tf_op jit(solution)/shard_map/reduce_scatter | solution.py:435
  1651.6 135.2 %reduce-scatter.48.cloned.1.call-start = ((), (), s32[]{:S(2)}) async-start(), calls=%async_computation.21 | async-start | bytes 2211840 | tf_op jit(solution)/shard_map/reduce_scatter | solution.py:438
  1657.6 158.2 %reduce-scatter.50.cloned.1.call-start = ((), (), s32[]{:S(2)}) async-start(), calls=%async_computation.22 | async-start | bytes 2211840 | tf_op jit(solution)/shard_map/reduce_scatter | solution.py:441
  1664.4 239.6 %all-reduce.11.cloned.1.call-start = ((), (), s32[]{:S(2)}) async-start(), calls=%async_computation.37 | async-start | bytes 299008 | tf_op jit(solution)/shard_map/psum | solution.py:446
  1665.3 150.6 %copy-start.56 = (bf16[4,64,576]{2,1,0:T(8,128)(2,1)S(1)}, bf16[4,64,576]{2,1,0:T(8,128)(2,1)}, u32[]{:S(2)}) copy-start(bf16[4,64,576]{2,1,0:T(8,128)(2,1)} %get-tuple-element.319) | copy-start | bytes 884740
  1665.6 150.4 %copy-start.9 = (bf16[1,1536,576]{1,2,0:T(8,128)(2,1)S(1)}, bf16[1,1536,576]{1,2,0:T(8,128)(2,1)}, u32[]{:S(2)}) copy-start(bf16[1,1536,576]{1,2,0:T(8,128)(2,1)} %all-gather.27.cloned.1.call-done) | copy-start | bytes 5308420
  1665.6 150.4 %copy-start.60 = (f32[64,576]{1,0:T(8,128)S(1)}, f32[64,576]{1,0:T(8,128)}, u32[]{:S(2)}) copy-start(f32[64,576]{1,0:T(8,128)} %copy-done.59) | copy-start | bytes 442372
  1667.8 148.2 %copy-start.145 = (bf16[64,1536]{1,0:T(8,128)(2,1)S(1)}, bf16[64,1536]{1,0:T(8,128)(2,1)}, u32[]{:S(2)}) copy-start(bf16[64,1536]{1,0:T(8,128)(2,1)} %get-tuple-element.78) | copy-start | bytes 589828
  1680.0 318.5 %all-reduce.13.cloned.1.call-start = ((), (), s32[]{:S(2)}) async-start(), calls=%async_computation.38 | async-start | bytes 3612672 | tf_op jit(solution)/shard_map/psum | solution.py:450
  1816.7 92.8 %copy-start.144 = (bf16[1,4,1,64,576]{4,3,1,2,0:T(8,128)(2,1)}, bf16[1,4,1,64,576]{4,3,1,2,0:T(8,128)(2,1)S(1)}, u32[]{:S(2)}) copy-start(bf16[1,4,1,64,576]{4,3,1,2,0:T(8,128)(2,1)S(1)} %fusion.239) | copy-start | bytes 884740
  1818.0 188.2 %copy-start.143 = (bf16[1,4,1,64,576]{4,3,1,2,0:T(8,128)(2,1)}, bf16[1,4,1,64,576]{4,3,1,2,0:T(8,128)(2,1)S(1)}, u32[]{:S(2)}) copy-start(bf16[1,4,1,64,576]{4,3,1,2,0:T(8,128)(2,1)S(1)} %fusion.527) | copy-start | bytes 884740
  (197 other events, 753.5 us)
Sparse Core Ops, SparseCore 0:
  9.7 31.3 all-gather.22
  42.8 28.0 all-gather.24
  72.6 31.4 all-gather.26
  638.5 68.9 reduce-scatter.51
  865.0 68.8 reduce-scatter.53
  963.1 72.3 reduce-scatter.55
  1039.0 71.5 reduce-scatter.57
  1138.5 72.2 reduce-scatter.59
  1214.4 71.5 reduce-scatter.61
  1313.8 72.3 reduce-scatter.63
  1389.7 71.4 reduce-scatter.65
  1484.4 72.2 reduce-scatter.67
  1560.8 71.4 reduce-scatter.69
  1635.1 20.4 reduce-scatter.41
  1657.8 20.5 reduce-scatter.43
  1681.3 22.0 reduce-scatter.71
  1706.2 22.0 reduce-scatter.39
  1730.6 26.7 reduce-scatter.45
  1759.9 26.7 reduce-scatter.47
  1789.0 26.7 reduce-scatter.49
  1820.5 83.3 all-reduce.10
  1909.0 89.5 all-reduce.12
where the time goes:
time: 2030 us; the launch traced here: 2010 us
  waiting for transfers between devices  901 us (44%)
  blocking collectives  565 us (28%)
  matrix products  226 us (11%)
  local copies, waits for them, and re-layouts  160 us (8%)
  other arithmetic  129 us (6%)
    unnamed x33, waiting for transfers between devices  615 us
    all_gather x5, blocking collectives, body(): all_values = lax.all_gather(kept_values, 'ctx', axis=0, tiled=True)  123 us
    all_gather x5, blocking collectives, body(): all_keys = lax.all_gather(kept_keys, 'ctx', axis=0, tiled=True)  122 us
    all_gather x5, blocking collectives, body(): lax.all_gather(key_row_block, 'ctx', axis=0, tiled=True)  121 us
    all_gather x5, blocking collectives, body(): lax.all_gather(value_row_block, 'ctx', axis=0, tiled=True)  120 us
    psum x1, waiting for transfers between devices, body(): lax.psum(shares[4].astype(jnp.bfloat16), 'ctx').astype(jnp.float32)  89.1 us
    psum x1, waiting for transfers between devices, body(): lax.psum(shares[0].astype(jnp.bfloat16), 'ctx').astype(jnp.float32)  85.9 us
    unnamed x509, local copies, waits for them, and re-layouts  79.4 us
  transfers between devices with their start and end apart: 30, of which 17 were waited for; matrix products, arithmetic and copies ran while one was open for 12% of the time, Pallas kernels for 0%

commit v1 on v0

v1 whole, which is shorter than its diff:
```python
import functools

import jax
import jax.numpy as jnp
from jax import lax
from jax.experimental import pallas as pl
from jax.experimental.pallas import tpu as pltpu
from jax.sharding import PartitionSpec as P

D = 576
HEADS = 9
KVH = 3
HD = 64
FF = 1536
ROWS = 64
TOK = 128
EPS = 1e-05
ROPE_BASE = 100000.0
FILL = -1e30
BF = jnp.bfloat16
F32 = jnp.float32
MESH = pl.DeviceIdType.MESH
VMEM = pltpu.VMEM
VLIM = 56 * 2**20


def mm(a, b):
    return jnp.dot(a, b, preferred_element_type=F32)


def mmt(a, b):
    return lax.dot_general(a, b, (((1,), (1,)), ((), ())), preferred_element_type=F32)


def tmm(a, b):
    return lax.dot_general(a, b, (((0,), (0,)), ((), ())), preferred_element_type=F32)


def place():
    c = lax.axis_index("ctx")
    return lax.axis_index("section"), c // 4, c % 4, lax.axis_index("fsdp")


def xp(x, y, d):
    return {"ctx": lax.rem(x + d, 4) * 4 + y}


def yp(x, y, d):
    return {"ctx": x * 4 + lax.rem(y + d, 4)}


def zp(z, d):
    return {"fsdp": lax.rem(z + d, 4)}


def greet(peers):
    barrier = pltpu.get_barrier_semaphore()
    for peer in peers:
        pl.semaphore_signal(barrier, inc=1, device_id=peer, device_id_type=MESH)
    pl.semaphore_wait(barrier, len(peers))


class Copies:
    def __init__(self, send, recv):
        self.send, self.recv, self.n = send, recv, 0
        self.all = []

    def push(self, src, dst, peer):
        i = self.n
        self.n += 1
        cp = pltpu.make_async_remote_copy(
            src_ref=src,
            dst_ref=dst,
            send_sem=self.send.at[i],
            recv_sem=self.recv.at[i],
            device_id=peer,
            device_id_type=MESH,
        )
        cp.start()
        self.all.append(cp)
        return cp

    def finish(self):
        for cp in self.all:
            cp.wait_send()


def xy_peers(x, y):
    return [xp(x, y, d) for d in (1, 2, 3)] + [yp(x, y, d) for d in (1, 2, 3)]


def weights_kernel(shard, w, send, recv, local):
    s, x, y, z = place()
    sib = {"section": 1 - s}
    greet(xy_peers(x, y) + [zp(z, d) for d in (1, 2, 3)] + [sib])
    cps = Copies(send, recv)
    zrows = pl.ds(pl.multiple_of(144 * z, 16), 144)
    own = pltpu.make_async_copy(shard.at[x, y], w.at[s, x, y, zrows], local)
    own.start()
    got = [
        cps.push(shard.at[x, y], w.at[s, x, y, zrows], zp(z, d)) for d in (1, 2, 3)
    ]
    own.wait()
    for cp in got:
        cp.wait_recv()
    ra, rb = pl.ds(0, 288), pl.ds(288, 288)
    got = []
    for d in (1, 2, 3):
        got.append(cps.push(w.at[s, x, y, ra], w.at[s, x, y, ra], xp(x, y, d)))
        got.append(cps.push(w.at[s, x, y, rb], w.at[s, x, y, rb], yp(x, y, d)))
    for cp in got:
        cp.wait_recv()
    got = []
    for d in (1, 2, 3):
        got.append(cps.push(w.at[s, :, y, ra], w.at[s, :, y, ra], yp(x, y, d)))
        got.append(cps.push(w.at[s, x, :, rb], w.at[s, x, :, rb], xp(x, y, d)))
    last = [
        cps.push(w.at[s, :, y, ra], w.at[s, :, y, ra], sib),
        cps.push(w.at[s, x, :, rb], w.at[s, x, :, rb], sib),
    ]
    for i, d in enumerate((1, 2, 3)):
        got[2 * i].wait_recv()
        fy = lax.rem(y + 4 - d, 4)
        last.append(cps.push(w.at[s, :, fy, ra], w.at[s, :, fy, ra], sib))
        got[2 * i + 1].wait_recv()
        fx = lax.rem(x + 4 - d, 4)
        last.append(cps.push(w.at[s, fx, :, rb], w.at[s, fx, :, rb], sib))
    for cp in last:
        cp.wait_recv()
    cps.finish()


def gather_weights(shard):
    n = 3 + 6 + 6 + 8
    return pl.pallas_call(
        weights_kernel,
        name="weights",
        out_shape=jax.ShapeDtypeStruct((2, 4, 4, D, 384), BF),
        in_specs=[pl.BlockSpec(memory_space=pl.ANY)],
        out_specs=pl.BlockSpec(memory_space=pl.ANY),
        scratch_shapes=[
            pltpu.SemaphoreType.DMA((n,)),
            pltpu.SemaphoreType.DMA((n,)),
            pltpu.SemaphoreType.DMA,
        ],
        compiler_params=pltpu.CompilerParams(collective_id=0, has_side_effects=True),
    )(shard)


def rope(v, cos, sin):
    lane = lax.broadcasted_iota(jnp.int32, v.shape, 1)
    turned = jnp.where(lane % 64 < 32, pltpu.roll(v, 96, 1), pltpu.roll(v, 32, 1))
    return v * cos + turned * sin


def kv_tables(cos, sin):
    lane = lax.broadcasted_iota(jnp.int32, cos.shape, 1)
    return jnp.where(lane < 64, cos, 1.0), jnp.where(lane < 64, sin, 0.0)


def low_lanes(v):
    lane = lax.broadcasted_iota(jnp.int32, v.shape, 1)
    return jnp.where(lane < 64, v, jnp.zeros_like(v))


def high_lanes(v):
    lane = lax.broadcasted_iota(jnp.int32, v.shape, 1)
    return jnp.where(lane < 64, jnp.zeros_like(v), v)


def inv_rms(v):
    return lax.rsqrt(jnp.mean(v * v, axis=-1, keepdims=True) + EPS)


def qkv_kernel(
    x_ref, gain_ref, w_ref, cos_ref, sin_ref, n1_ref, q_ref, kv_ref, send, recv
):
    s, x, y, z = place()
    v = x_ref[...].astype(F32)
    n1 = (v * inv_rms(v) * gain_ref[...]).astype(BF)
    n1_ref[...] = n1
    cos, sin = cos_ref[...], sin_ref[...]
    ckv, skv = kv_tables(cos, sin)
    kv = mm(n1, w_ref[3])
    for j in range(KVH):
        blk = rope(kv[:, 128 * j : 128 * j + 128], ckv, skv).astype(BF)
        for m in range(2):
            kv_ref[m, x, y, :, 128 * j : 128 * j + 128] = blk[64 * m : 64 * m + 64]
    greet(xy_peers(x, y))
    cps = Copies(send, recv)
    got = []
    for d in (1, 2, 3):
        got.append(cps.push(kv_ref.at[0, x, y], kv_ref.at[0, x, y], xp(x, y, d)))
        got.append(cps.push(kv_ref.at[1, x, y], kv_ref.at[1, x, y], yp(x, y, d)))
    qq = [mm(n1, w_ref[0]), mm(n1, w_ref[1][:, :256])]
    q = jnp.concatenate(qq, axis=1) * 0.125
    for b in range(5):
        blk = rope(q[:, 128 * b : 128 * b + 128], cos, sin)
        for half in range(2):
            h = 2 * b + half
            if h >= HEADS:
                continue
            part = low_lanes(blk if half == 0 else pltpu.roll(blk, 64, 1)).astype(BF)
            j, g = h // 3, h % 3
            for m in range(2):
                q_ref[3 * m + j, 64 * g : 64 * g + 64] = part[64 * m : 64 * m + 64]
    for cp in got:
        cp.wait_recv()
    got = []
    for d in (1, 2, 3):
        got.append(cps.push(kv_ref.at[0, :, y], kv_ref.at[0, :, y], yp(x, y, d)))
        got.append(cps.push(kv_ref.at[1, x], kv_ref.at[1, x], xp(x, y, d)))
    for cp in got:
        cp.wait_recv()
    cps.finish()


def vm():
    return pl.BlockSpec(memory_space=pltpu.VMEM)


def hbm():
    return pl.BlockSpec(memory_space=pl.ANY)


def qkv_call(layer, xin, gain, w, cos, sin):
    return pl.pallas_call(
        qkv_kernel,
        name="qkv",
        grid=(1,),
        out_shape=(
            jax.ShapeDtypeStruct((TOK, D), BF),
            jax.ShapeDtypeStruct((6, 192, 128), BF),
            jax.ShapeDtypeStruct((2, 4, 4, ROWS, 384), BF),
        ),
        in_specs=[
            vm(),
            vm(),
            pl.BlockSpec((None, 4, D, 384), lambda i: (layer, 0, 0, 0)),
            vm(),
            vm(),
        ],
        out_specs=(vm(), vm(), vm()),
        scratch_shapes=[
            pltpu.SemaphoreType.DMA((12,)),
            pltpu.SemaphoreType.DMA((12,)),
        ],
        compiler_params=pltpu.CompilerParams(
            collective_id=1 + layer, has_side_effects=True, vmem_limit_bytes=VLIM
        ),
    )(xin, gain, w, cos, sin)


def fwd_kernel(
    x_ref, q_ref, kv_ref, qpos_ref, kpos_ref, gain_ref, w_hbm,
    act_ref, h_ref, o_ref, p_ref, g_ref, u_ref, m_ref,
    w_ref, sem,
):
    layer = sem[1]
    loads = [
        pltpu.make_async_copy(w_hbm.at[layer, 1 + 0], w_ref.at[0], sem[0].at[0]),
        pltpu.make_async_copy(w_hbm.at[layer, 2], w_ref.at[1], sem[0].at[1]),
        pltpu.make_async_copy(
            w_hbm.at[layer, pl.ds(4, 12)], w_ref.at[pl.ds(2, 12)], sem[0].at[2]
        ),
    ]
    for cp in loads:
        cp.start()
    heads = {}
    for m in range(2):
        allowed = kpos_ref[m : m + 1, :] <= qpos_ref[m]
        for j in range(KVH):
            kvb = kv_ref[m, :, 128 * j : 128 * j + 128]
            sc = jnp.where(allowed, mmt(q_ref[3 * m + j], kvb), FILL)
            e = jnp.exp(sc - jnp.max(sc, axis=-1, keepdims=True))
            p = (e * (1.0 / jnp.sum(e, axis=-1, keepdims=True))).astype(BF)
            p_ref[3 * m + j] = p
            o = mm(p, kvb)
            for g in range(3):
                heads[m, 3 * j + g] = o[64 * g : 64 * g + 64]
        for b in range(5):
            hi = high_lanes(heads[m, 2 * b])
            if b > 0:
                hi = hi + low_lanes(pltpu.roll(heads[m, 2 * b - 1], 64, 1))
            o_ref[64 * m : 64 * m + 64, 128 * b : 128 * b + 128] = hi.astype(BF)
    for cp in loads:
        cp.wait()
    ob = o_ref[...]
    h = x_ref[...].astype(F32) + (
        mmt(ob[:, :256], w_ref[0][:, 128:384]) + mmt(ob[:, 256:], w_ref[1])
    )
    h_ref[...] = h
    n2 = (h * inv_rms(h) * gain_ref[...]).astype(BF)
    acc = h
    for i in range(4):
        cols = slice(384 * i, 384 * i + 384)
        g = mm(n2, w_ref[2 + i])
        u = mm(n2, w_ref[6 + i])
        g_ref[:, cols] = g
        u_ref[:, cols] = u
        low = (g * jax.nn.sigmoid(g) * u).astype(BF)
        m_ref[:, cols] = low
        acc = acc + mmt(low, w_ref[10 + i])
    act_ref[...] = acc.astype(BF)


def fwd_call(layer, xin, q, kv, qpos, kpos, gain, w):
    def kernel(*refs):
        fwd_kernel(*refs[:-1], (refs[-1], layer))

    return pl.pallas_call(
        kernel,
        name="forward",
        out_shape=(
            jax.ShapeDtypeStruct((TOK, D), BF),
            jax.ShapeDtypeStruct((TOK, D), F32),
            jax.ShapeDtypeStruct((TOK, 640), BF),
            jax.ShapeDtypeStruct((6, 192, 1024), BF),
            jax.ShapeDtypeStruct((TOK, FF), F32),
            jax.ShapeDtypeStruct((TOK, FF), F32),
            jax.ShapeDtypeStruct((TOK, FF), BF),
        ),
        in_specs=[vm()] * 6 + [hbm()],
        out_specs=(vm(),) * 7,
        scratch_shapes=[VMEM((14, D, 384), BF), pltpu.SemaphoreType.DMA((3,))],
        compiler_params=pltpu.CompilerParams(vmem_limit_bytes=VLIM),
    )(xin, q, kv, qpos, kpos, gain, w)


def bwd_kernel(
    layer, dy_ref, h_ref, p_ref, g_ref, u_ref, m_ref, q_ref, kv_ref, gain_ref,
    cos_ref, sin_ref, w_hbm, *rest,
):
    dh_ref, dq_ref, dkv_ref, gg_ref, grads, w_ref, gbuf, wsem, gsem = rest[-9:]
    loads = [
        pltpu.make_async_copy(
            w_hbm.at[layer, pl.ds(4, 12)], w_ref.at[pl.ds(2, 12)], wsem.at[2]
        ),
        pltpu.make_async_copy(w_hbm.at[layer, pl.ds(1, 2)], w_ref.at[pl.ds(0, 2)], wsem.at[0]),
    ]
    for cp in loads:
        cp.start()
    dyb = dy_ref[...]
    h = h_ref[...]
    r = inv_rms(h)
    gain = gain_ref[...]
    n2 = (h * r * gain).astype(BF)
    dyt = dyb.T
    n2t = n2.T
    loads[0].wait()
    dn2 = jnp.zeros((TOK, D), F32)
    outs = []
    for i in range(4):
        cols = slice(384 * i, 384 * i + 384)
        dm = mm(dyb, w_ref[10 + i])
        g = g_ref[:, cols]
        u = u_ref[:, cols]
        sg = jax.nn.sigmoid(g)
        dg = (dm * u * sg * (1.0 + g * (1.0 - sg))).astype(BF)
        du = (dm * g * sg).astype(BF)
        gbuf[0, i] = mm(n2t, dg).astype(BF)
        gbuf[1, i] = mm(n2t, du).astype(BF)
        gbuf[2, i] = mm(dyt, m_ref[:, cols]).astype(BF)
        for k in range(3):
            cp = pltpu.make_async_copy(
                gbuf.at[k, i], grads.at[layer, 1 + k, i], gsem.at[3 * i + k]
            )
            cp.start()
            outs.append(cp)
        dn2 = dn2 + mmt(dg, w_ref[2 + i]) + mmt(du, w_ref[6 + i])
    scaled = dn2 * gain
    inner = jnp.mean(scaled * h, axis=-1, keepdims=True)
    dh = dyb.astype(F32) + (r * scaled - h * (r * r * r) * inner)
    gg_ref[...] = jnp.sum(dn2 * h * r, axis=0, keepdims=True)
    dh_ref[...] = dh
    dhb = dh.astype(BF)
    loads[1].wait()
    do = jnp.concatenate([mm(dhb, w_ref[0][:, 128:384]), mm(dhb, w_ref[1])], axis=1)
    dqs = {}
    for m in range(2):
        for j in range(KVH):
            kvb = kv_ref[m, :, 128 * j : 128 * j + 128]
            parts = []
            for g in range(3):
                hh = 3 * j + g
                b = (hh + 1) // 2
                blk = do[64 * m : 64 * m + 64, 128 * b : 128 * b + 128]
                parts.append(
                    high_lanes(blk if hh % 2 == 0 else pltpu.roll(blk, 64, 1))
                )
            dop = jnp.concatenate(parts, axis=0).astype(BF)
            pb = p_ref[3 * m + j]
            p = pb.astype(F32)
            dp = mmt(dop, kvb)
            delta = jnp.sum(p * dp, axis=-1, keepdims=True)
            ds = (p * (dp - delta)).astype(BF)
            dq = mm(ds, kvb) * 0.125
            for g in range(3):
                dqs[m, 3 * j + g] = dq[64 * g : 64 * g + 64]
            dkvt = mm(q_ref[3 * m + j].T, ds) + mm(dop.T, pb)
            dkv_ref[m, :, 128 * j : 128 * j + 128] = dkvt.T.astype(BF)
        cos, sin = cos_ref[64 * m : 64 * m + 64], sin_ref[64 * m : 64 * m + 64]
        for b in range(5):
            blk = low_lanes(dqs[m, 2 * b])
            if 2 * b + 1 < HEADS:
                blk = blk + high_lanes(pltpu.roll(dqs[m, 2 * b + 1], 64, 1))
            dq_ref[64 * m : 64 * m + 64, 128 * b : 128 * b + 128] = rope(
                blk, cos, -sin
            ).astype(BF)
    for cp in outs:
        cp.wait()


def bwd_call(layer, dy, h, p, g, u, m, q, kv, gain, cos, sin, w, grads):
    started = [] if grads is None else [grads]
    return pl.pallas_call(
        functools.partial(bwd_kernel, layer),
        name="backward",
        out_shape=(
            jax.ShapeDtypeStruct((TOK, D), F32),
            jax.ShapeDtypeStruct((TOK, 640), BF),
            jax.ShapeDtypeStruct((2, 1024, 384), BF),
            jax.ShapeDtypeStruct((1, D), F32),
            jax.ShapeDtypeStruct((2, 4, 4, D, 384), BF),
        ),
        in_specs=[vm()] * 11 + [hbm()] * (1 + len(started)),
        out_specs=(vm(), vm(), vm(), vm(), hbm()),
        scratch_shapes=[
            VMEM((14, D, 384), BF),
            VMEM((3, 4, D, 384), BF),
            pltpu.SemaphoreType.DMA((3,)),
            pltpu.SemaphoreType.DMA((12,)),
        ],
        input_output_aliases={12: 4} if started else {},
        compiler_params=pltpu.CompilerParams(vmem_limit_bytes=VLIM),
    )(dy, h, p, g, u, m, q, kv, gain, cos, sin, w, *started)


def dkv_kernel(
    layer, part_ref, n1_ref, dq_ref, o_ref, dh_ref, x_ref, gain_ref, w_ref,
    cos_ref, sin_ref, grads_in,
    dx_ref, gg_ref, grads,
    got1, got2, mid, gbuf, send, recv, gsem,
):
    s, x, y, z = place()
    greet(xy_peers(x, y))
    cps = Copies(send, recv)
    one = []
    for d in (1, 2, 3):
        ty, tx = lax.rem(y + d, 4), lax.rem(x + d, 4)
        one.append(cps.push(part_ref.at[0, :, ty], got1.at[0, d - 1], yp(x, y, d)))
        one.append(cps.push(part_ref.at[1, tx], got1.at[1, d - 1], xp(x, y, d)))
    n1 = n1_ref[...]
    dqb = dq_ref[...]
    dh = dh_ref[...]
    ob = o_ref[...]
    zero = jnp.zeros((TOK, 512), BF)
    left = jnp.concatenate([n1, dh.astype(BF)], axis=0).T
    right = jnp.concatenate(
        [jnp.concatenate([dqb, zero], axis=1), jnp.concatenate([zero, ob], axis=1)],
        axis=0,
    )
    outs = []
    for i in range(3):
        gbuf[i] = mm(left, right[:, 384 * i : 384 * i + 384]).astype(BF)
        cp = pltpu.make_async_copy(gbuf.at[i], grads.at[layer, 0, i], gsem.at[i])
        cp.start()
        outs.append(cp)
    dn1 = mmt(dqb[:, :384], w_ref[0]) + mmt(dqb[:, 384:], w_ref[1][:, :256])
    for cp in one:
        cp.wait_recv()
    for i in range(4):
        a = part_ref[0, i, y].astype(F32)
        b = part_ref[1, x, i].astype(F32)
        for d in range(3):
            a = a + got1[0, d, i].astype(F32)
            b = b + got1[1, d, i].astype(F32)
        mid[0, i] = a.astype(BF)
        mid[1, i] = b.astype(BF)
    two = []
    for d in (1, 2, 3):
        ty, tx = lax.rem(y + d, 4), lax.rem(x + d, 4)
        two.append(cps.push(mid.at[0, tx], got2.at[0, d - 1], xp(x, y, d)))
        two.append(cps.push(mid.at[1, ty], got2.at[1, d - 1], yp(x, y, d)))
    for cp in two:
        cp.wait_recv()
    a = mid[0, x].astype(F32)
    b = mid[1, y].astype(F32)
    for d in range(3):
        a = a + got2[0, d].astype(F32)
        b = b + got2[1, d].astype(F32)
    total = jnp.concatenate([a, b], axis=0)
    ckv, skv = kv_tables(cos_ref[...], -sin_ref[...])
    dkv = jnp.concatenate(
        [rope(total[:, 128 * j : 128 * j + 128], ckv, skv) for j in range(KVH)], axis=1
    ).astype(BF)
    gbuf[3] = tmm(n1, dkv).astype(BF)
    cp = pltpu.make_async_copy(gbuf.at[3], grads.at[layer, 0, 3], gsem.at[3])
    cp.start()
    outs.append(cp)
    dn1 = dn1 + mmt(dkv, w_ref[3])
    v = x_ref[...].astype(F32)
    r = inv_rms(v)
    scaled = dn1 * gain_ref[...]
    inner = jnp.mean(scaled * v, axis=-1, keepdims=True)
    dx_ref[...] = (dh + (r * scaled - v * (r * r * r) * inner)).astype(BF)
    gg_ref[...] = jnp.sum(dn1 * v * r, axis=0, keepdims=True)
    for cp in outs:
        cp.wait()
    cps.finish()


def dkv_call(layer, part, n1, dq, o, dh, xin, gain, w, cos, sin, grads):
    return pl.pallas_call(
        functools.partial(dkv_kernel, layer),
        name="dkv",
        grid=(1,),
        out_shape=(
            jax.ShapeDtypeStruct((TOK, D), BF),
            jax.ShapeDtypeStruct((1, D), F32),
            jax.ShapeDtypeStruct(grads.shape, BF),
        ),
        in_specs=[vm()] * 7
        + [pl.BlockSpec((None, 4, D, 384), lambda i: (layer, 0, 0, 0))]
        + [vm()] * 2
        + [hbm()],
        out_specs=(vm(), vm(), hbm()),
        scratch_shapes=[
            VMEM((2, 3, 4, ROWS, 384), BF),
            VMEM((2, 3, ROWS, 384), BF),
            VMEM((2, 4, ROWS, 384), BF),
            VMEM((4, D, 384), BF),
            pltpu.SemaphoreType.DMA((12,)),
            pltpu.SemaphoreType.DMA((12,)),
            pltpu.SemaphoreType.DMA((4,)),
        ],
        input_output_aliases={10: 2},
        compiler_params=pltpu.CompilerParams(
            collective_id=3 + layer, has_side_effects=True, vmem_limit_bytes=VLIM
        ),
    )(part, n1, dq, o, dh, xin, gain, w, cos, sin, grads)


def add_into(dst, srcs, chunk=96):
    rows = dst.shape[0]

    def step(i, carry):
        at = pl.ds(pl.multiple_of(i * chunk, 16), chunk)
        total = dst[at].astype(F32)
        for src in srcs:
            total = total + src[at].astype(F32)
        dst[at] = total.astype(BF)
        return carry

    lax.fori_loop(0, rows // chunk, step, 0)


def reduce_kernel(
    grads, gains, pairs, out, gout, pout,
    hold, sib_in, ra_in, rb_in, r2a, r2b, fin, r3, gsum, gin, send, recv, lsem,
):
    s, x, y, z = place()
    sib = {"section": 1 - s}
    peers = xy_peers(x, y) + [zp(z, d) for d in (1, 2, 3)] + [sib]
    greet(peers)
    cps = Copies(send, recv)
    ra, rb = pl.ds(0, 288), pl.ds(288, 288)
    own = pltpu.make_async_copy(grads.at[s], hold, lsem.at[0])
    own.start()
    mine = pltpu.make_async_copy(gains.at[s], gsum, lsem.at[1])
    mine.start()
    half = [
        cps.push(grads.at[1 - s, i], sib_in.at[i], sib) for i in range(4)
    ]
    gcp = cps.push(gains.at[1 - s], gin.at[9], sib)
    pcp = cps.push(pairs.at[1 - s], pout, sib)
    own.wait()
    mine.wait()
    for i in range(4):
        half[i].wait_recv()
        for k in range(4):
            add_into(hold.at[i, k], [sib_in.at[i, k]])
    gcp.wait_recv()
    gsum[...] = gsum[...] + gin[9]
    one, gone = [], []
    for d in (1, 2, 3):
        tx, ty = lax.rem(x + d, 4), lax.rem(y + d, 4)
        one.append(cps.push(hold.at[tx, :, ra], ra_in.at[d - 1], xp(x, y, d)))
        one.append(cps.push(hold.at[:, ty, rb], rb_in.at[d - 1], yp(x, y, d)))
        gone.append(cps.push(gsum, gin.at[d - 1], xp(x, y, d)))
    for cp in one + gone:
        cp.wait_recv()
    for cp in gone:
        cp.wait_send()
        cps.all = [other for other in cps.all if other is not cp]
    for k in range(4):
        add_into(hold.at[x, k, ra], [ra_in.at[d, k] for d in range(3)])
        add_into(hold.at[k, y, rb], [rb_in.at[d, k] for d in range(3)])
    gsum[...] = gsum[...] + gin[0] + gin[1] + gin[2]
    two, gone = [], []
    for d in (1, 2, 3):
        tx, ty = lax.rem(x + d, 4), lax.rem(y + d, 4)
        two.append(cps.push(hold.at[x, ty, ra], r2a.at[d - 1], yp(x, y, d)))
        two.append(cps.push(hold.at[tx, y, rb], r2b.at[d - 1], xp(x, y, d)))
        gone.append(cps.push(gsum, gin.at[2 + d], yp(x, y, d)))
    for cp in two + gone:
        cp.wait_recv()
    for cp in gone:
        cp.wait_send()
        cps.all = [other for other in cps.all if other is not cp]
    add_into(hold.at[x, y, ra], [r2a.at[d] for d in range(3)])
    add_into(hold.at[x, y, rb], [r2b.at[d] for d in range(3)])
    gsum[...] = gsum[...] + gin[3] + gin[4] + gin[5]
    three, gone = [], []
    for d in (1, 2, 3):
        tz = pl.ds(pl.multiple_of(lax.rem(z + d, 4) * 144, 16), 144)
        three.append(cps.push(hold.at[x, y, tz], r3.at[d - 1], zp(z, d)))
        gone.append(cps.push(gsum, gin.at[5 + d], zp(z, d)))
    for cp in three + gone:
        cp.wait_recv()
    gout[...] = gsum[...] + gin[6] + gin[7] + gin[8]
    mz = pl.ds(pl.multiple_of(z * 144, 16), 144)
    total = hold[x, y, mz].astype(F32)
    for d in range(3):
        total = total + r3[d].astype(F32)
    out[x, y] = total.astype(BF)
    qa, qb = pl.ds(0, 80), pl.ds(80, 64)
    four = []
    for d in (1, 2, 3):
        four.append(cps.push(out.at[x, y, qa], out.at[x, y, qa], xp(x, y, d)))
        four.append(cps.push(out.at[x, y, qb], out.at[x, y, qb], yp(x, y, d)))
    for cp in four:
        cp.wait_recv()
    five = []
    for d in (1, 2, 3):
        five.append(cps.push(out.at[:, y, qa], out.at[:, y, qa], yp(x, y, d)))
        five.append(cps.push(out.at[x, :, qb], out.at[x, :, qb], xp(x, y, d)))
    for cp in five + [pcp]:
        cp.wait_recv()
    cps.finish()


def reduce_call(grads, gains, pairs):
    n = 6 + 9 + 9 + 6 + 6 + 6
    return pl.pallas_call(
        reduce_kernel,
        name="reduce",
        out_shape=(
            jax.ShapeDtypeStruct((4, 4, 144, 384), BF),
            jax.ShapeDtypeStruct((8, D), F32),
            jax.ShapeDtypeStruct((2, TOK, D), BF),
        ),
        in_specs=[hbm(), vm(), vm()],
        out_specs=(vm(), vm(), vm()),
        scratch_shapes=[
            VMEM((4, 4, D, 384), BF),
            VMEM((4, 4, D, 384), BF),
            VMEM((3, 4, 288, 384), BF),
            VMEM((3, 4, 288, 384), BF),
            VMEM((3, 288, 384), BF),
            VMEM((3, 288, 384), BF),
            VMEM((144, 384), BF),
            VMEM((3, 144, 384), BF),
            VMEM((8, D), F32),
            VMEM((10, 8, D), F32),
            pltpu.SemaphoreType.DMA((n,)),
            pltpu.SemaphoreType.DMA((n,)),
            pltpu.SemaphoreType.DMA((2,)),
        ],
        compiler_params=pltpu.CompilerParams(
            collective_id=5, has_side_effects=True, vmem_limit_bytes=VLIM
        ),
    )(grads, gains, pairs)


def pack(w_query, key_weight, value_weight, w_out, w_gate, w_up, w_down):
    kv = jnp.concatenate(
        [key_weight.reshape(144, 3, 64), value_weight.reshape(144, 3, 64)], axis=2
    ).reshape(144, 384)
    flat = jnp.concatenate([w_query, w_out.T, kv, w_gate, w_up, w_down.T], axis=1)
    return flat.reshape(144, 16, 384).transpose(1, 0, 2).reshape(4, 4, 144, 384)


def body(
    inputs, piece_order, cotangent, gain_attn, w_query, key_weight, value_weight,
    w_out, gain_mlp, w_gate, w_up, w_down,
):
    s = lax.axis_index("section")
    c = lax.axis_index("ctx")
    z = lax.axis_index("fsdp")
    shard = pack(
        w_query[0], key_weight[0], value_weight[0], w_out[0], w_gate[0], w_up[0], w_down[0]
    )
    w5 = gather_weights(shard)
    w = w5.reshape(2, 16, D, 384)
    gains = lax.all_gather(
        jnp.concatenate([gain_attn, gain_mlp], axis=0), ("section", "fsdp"), axis=0
    )
    gains = gains.reshape(2, 4, 2, 144).transpose(0, 2, 1, 3).reshape(2, 2, 1, D)
    gains = gains.astype(F32)

    order = lax.dynamic_slice_in_dim(piece_order[:, 0], 2 * s, 2, 0)
    kpos = (order[:, :, None] * 32 + jnp.arange(32, dtype=jnp.int32)).reshape(2, 1024)
    lpos = lax.dynamic_slice_in_dim(kpos, c * ROWS, ROWS, 1)
    qpos = jnp.tile(lpos, (1, 3)).reshape(2, 192, 1)
    frequency = ROPE_BASE ** (-jnp.arange(32, dtype=F32) / 32)
    angles = lpos.reshape(TOK, 1).astype(F32) * frequency[None, :]
    cos1, sin1 = jnp.cos(angles), jnp.sin(angles)
    cos = jnp.concatenate([cos1] * 4, axis=1)
    sin = jnp.concatenate([-sin1, sin1, -sin1, sin1], axis=1)

    x1 = lax.dynamic_slice_in_dim(inputs[:, 0], 2 * s, 2, 0).reshape(TOK, D)
    cot = lax.dynamic_slice_in_dim(cotangent[:, 0], 2 * s, 2, 0).reshape(TOK, D)

    xs, kept = [x1], []
    for layer in range(2):
        n1, q, kv = qkv_call(layer, xs[layer], gains[layer, 0], w, cos, sin)
        kv = kv.reshape(2, 1024, 384)
        act, h, o, p, g, u, m = fwd_call(
            layer, xs[layer], q, kv, qpos, kpos, gains[layer, 1], w
        )
        xs.append(act)
        kept.append((n1, q, kv, h, o, p, g, u, m))
    dy = cot
    grads = None
    dxs, ggs = [None, None], [None, None]
    for layer in (1, 0):
        n1, q, kv, h, o, p, g, u, m = kept[layer]
        dh, dq, dkv, gg2, grads = bwd_call(
            layer, dy, h, p, g, u, m, q, kv, gains[layer, 1], cos, sin, w, grads
        )
        dy, gg1, grads = dkv_call(
            layer, dkv.reshape(2, 4, 4, ROWS, 384), n1, dq, o, dh, xs[layer],
            gains[layer, 0], w, cos, sin, grads,
        )
        dxs[layer] = dy
        ggs[layer] = jnp.concatenate([gg1, gg2, jnp.zeros((6, D), F32)], axis=0)
    pairs = jnp.stack([jnp.stack([xs[l + 1], dxs[l]]) for l in range(2)])
    red, gsum, other = reduce_call(grads, jnp.stack(ggs), pairs)

    own = lax.dynamic_index_in_dim(pairs, s, 0, keepdims=False).reshape(2, 2, ROWS, D)
    other = other.reshape(2, 2, ROWS, D)
    first = s == 0
    both = jnp.concatenate(
        [jnp.where(first, own, other), jnp.where(first, other, own)], axis=1
    )
    flat = red.reshape(16, 144, 384).transpose(1, 0, 2).reshape(144, 6144).astype(F32)
    gsh = lax.dynamic_slice_in_dim(gsum, z * 144, 144, 1)
    kvg = flat[:, 1152:1536].reshape(144, 3, 2, 64)
    return (
        both[0][None, :, None],
        both[1][None, :, None],
        gsh[0:1],
        flat[None, :, 0:576],
        kvg[:, :, 0].reshape(1, 144, 192),
        kvg[:, :, 1].reshape(1, 144, 192),
        flat[:, 576:1152].T[None],
        gsh[1:2],
        flat[None, :, 1536:3072],
        flat[None, :, 3072:4608],
        flat[:, 4608:6144].T[None],
    )


def solution(mesh):
    placed = (
        P(None, "fsdp", "ctx", None),
        P(None, "fsdp", None),
        P(None, "fsdp", "ctx", None),
        P("section", "fsdp"),
        P("section", "fsdp", None),
        P("section", "fsdp", None),
        P("section", "fsdp", None),
        P("section", None, "fsdp"),
        P("section", "fsdp"),
        P("section", "fsdp", None),
        P("section", "fsdp", None),
        P("section", None, "fsdp"),
    )
    return jax.shard_map(
        body,
        mesh=mesh,
        in_specs=placed,
        out_specs=(
            P("section", None, "fsdp", "ctx", None),
            P("section", None, "fsdp", "ctx", None),
            P("section", "fsdp"),
            P("section", "fsdp", None),
            P("section", "fsdp", None),
            P("section", "fsdp", None),
            P("section", None, "fsdp"),
            P("section", "fsdp"),
            P("section", "fsdp", None),
            P("section", "fsdp", None),
            P("section", None, "fsdp"),
        ),
        check_vma=False,
    )
```

time: 2030 us -> 355 us (0.17)
  waiting for transfers between devices: 901 us -> 0 us
  blocking collectives: 565 us -> 15 us
  Pallas kernels: 0 us -> 302 us
  matrix products: 226 us -> 0 us
  local copies, waits for them, and re-layouts: 160 us -> 26.7 us
  other arithmetic: 129 us -> 10.1 us
    unnamed x33 -> x0, waiting for transfers between devices: 615 us -> none
    all_gather x24 -> x1, blocking collectives: 543 us -> 15 us  [body(): lax.all_gather(jnp.concatenate([gain_attn, gain_mlp], axis=0), ('section'...]
    pallas_call x0 -> x10, Pallas kernels: none -> 302 us  [the longest x1 96.8 us: reduce_call(): pl.pallas_call(reduce_kernel, name='reduce', out_shape=(jax.ShapeDtypeStr...]
    dot_general x140 -> x0, matrix products: 226 us -> none  [the longest x35 52.6 us: trans_times(): lax.dot_general(first_op, second_op, (((0,), (0,)), ((), ())), preferred_...]
    psum x2 -> x0, waiting for transfers between devices: 175 us -> none  [the longest x1 89.1 us: body(): lax.psum(shares[4].astype(jnp.bfloat16), 'ctx').astype(jnp.float32)]
    reduce_scatter x6 -> x0, waiting for transfers between devices: 111 us -> none  [the longest x1 29.4 us: body(): lax.psum_scatter(total_up.astype(jnp.bfloat16), 'fsdp', scatter_dimension...]
    unnamed x509 -> x26, local copies, waits for them, and re-layouts: 79.4 us -> 6.03 us
    all_gather x20 -> x0, local copies, waits for them, and re-layouts: 36.8 us -> none  [the longest x5 9.96 us: body(): all_keys = lax.all_gather(kept_keys, 'ctx', axis=0, tiled=True)]
  transfers between devices with their start and end apart: 30 -> 0, of which waited for: 17 -> 0; matrix products, arithmetic and copies ran while one was open for 12% -> 0% of each run, Pallas kernels for 0% -> 0%
where the time goes in v1:
time: 355 us; the launch traced here: 354 us
  Pallas kernels  302 us (85%)
  local copies, waits for them, and re-layouts  26.7 us (8%)
  blocking collectives  15 us (4%)
  other arithmetic  10.1 us (3%)
    pallas_call x1, Pallas kernels, reduce_call(): pl.pallas_call(reduce_kernel, name='reduce', out_shape=(jax.ShapeDtypeStr...  96.8 us
    pallas_call x1, Pallas kernels, gather_weights(): pl.pallas_call(weights_kernel, name='weights', out_shape=jax.ShapeDtypeSt...  70.9 us
    pallas_call x2, Pallas kernels, dkv_call(): pl.pallas_call(functools.partial(dkv_kernel, layer), name='dkv', grid=(1,...  42 us
    pallas_call x2, Pallas kernels, qkv_call(): pl.pallas_call(qkv_kernel, name='qkv', grid=(1,), out_shape=(jax.ShapeDty...  40.1 us
    pallas_call x2, Pallas kernels, bwd_call(): pl.pallas_call(functools.partial(bwd_kernel, layer), name='backward', out...  29.4 us
    pallas_call x2, Pallas kernels, fwd_call(): pl.pallas_call(kernel, name='forward', out_shape=(jax.ShapeDtypeStruct((T...  22.3 us
    all_gather x1, blocking collectives, body(): lax.all_gather(jnp.concatenate([gain_attn, gain_mlp], axis=0), ('section'...  15 us

profile of v1, /device:TPU:0, one launch (start us, length us, event | category | flops | bytes accessed | tf_op | source)
XLA Modules:
  0.0 354.4 jit_solution(5097698468472857465)
XLA Ops:
  0.6 0.7 fusion.5
  1.3 0.1 add.36
  1.4 0.1 add.37
  1.5 0.1 add.39
  1.6 0.1 fusion.6
  1.7 0.1 convert_element_type.48
  1.8 0.3 fusion.4
  2.1 0.8 pad_maximum_fusion.3
  2.9 1.7 constant_dynamic-slice_fusion.1
  4.7 1.0 copy.53
  5.6 1.0 copy.54
  6.7 0.1 copy.65
  6.8 2.7 concatenate.26
  9.5 1.4 copy.70
  10.9 0.0 copy-done.5
  10.9 70.9 %weights.1 = bf16[2,4,4,576,384]{4,3,2,1,0:T(8,128)(2,1)} custom-call(bf16[4,4,144,384]{3,2,1,0:T(8,128)(2,1)} %bitcast.95), custom_call_target="tpu_custom_call" | custom-call | tf_op jit(solution)/shard_map/weights/pallas_call | solution.py:135
  81.8 0.0 copy-done.9
  81.8 0.0 copy-done.10
  81.9 15.0 %all-gather.1 = bf16[8,2,144]{2,1,0:T(2,128)(2,1)S(1)} all-gather(bf16[1,2,144]{2,1,0:T(2,128)(2,1)S(1)} %maximum_bitcast_fusion.4), channel_id=2, replica_groups=mesh['section'=2,'ctx'=16,'fsdp'=4] {'section','fsdp'}, dimensions={0}, use_global_device_ids=true | all-gather | bytes 5184 | tf_op jit(solution)/shard_map/all_gather | solution.py:696
  96.9 0.1 reshape.138
  97.0 0.6 slice_bitcast_fusion.5
  97.6 21.4 %qkv.2 = (bf16[128,576]{1,0:T(8,128)(2,1)}, bf16[6,192,128]{2,1,0:T(8,128)(2,1)}, bf16[2,4,4,64,384]{4,3,2,1,0:T(8,128)(2,1)}) custom-call(bf16[128,576]{1,0:T(8,128)(2,1)} %bitcast.101, f32[1,576]{1,0:T(1,128)} %get-tuple-element.140.gain_ref, bf16[2,16,576,384]{3,2,1,0:T(8,128)(2,1)} %bitcast.83, f32[128,128]{1,0:T(8,128)} %get-tuple-element.148.cos_ref, ...), custom_call_target="tpu_custom_call" | custom-call | tf_op jit(solution)/shard_map/qkv/pallas_call | solution.py:227
  119.0 0.9 tile.10.refs_3_
  119.8 11.2 %forward.2 = (bf16[128,576]{1,0:T(8,128)(2,1)}, f32[128,576]{1,0:T(8,128)}, bf16[128,640]{1,0:T(8,128)(2,1)}, bf16[6,192,1024]{2,1,0:T(8,128)(2,1)}, f32[128,153...) custom-call(bf16[128,576]{1,0:T(8,128)(2,1)} %bitcast.102, ...), custom_call_target="tpu_custom_call" | custom-call | tf_op jit(solution)/shard_map/forward/pallas_call | solution.py:311
  131.0 18.8 %qkv.3 = (bf16[128,576]{1,0:T(8,128)(2,1)}, bf16[6,192,128]{2,1,0:T(8,128)(2,1)}, bf16[2,4,4,64,384]{4,3,2,1,0:T(8,128)(2,1)}) custom-call(bf16[128,576]{1,0:T(8,128)(2,1)} %get-tuple-element.52.x_ref.refs_0_, f32[1,576]{1,0:T(1,128)} %get-tuple-element.138.gain_ref, bf16[2,16,576,384]{3,2,1,0:T(8,128)(2,1)} %bitcast.85, ...), custom_call_target="tpu_custom_call" | custom-call | tf_op jit(solution)/shard_map/qkv/pallas_call | solution.py:227
  149.8 11.1 %forward.3 = (bf16[128,576]{1,0:T(8,128)(2,1)}, f32[128,576]{1,0:T(8,128)}, bf16[128,640]{1,0:T(8,128)(2,1)}, bf16[6,192,1024]{2,1,0:T(8,128)(2,1)}, f32[128,153...) custom-call(bf16[128,576]{1,0:T(8,128)(2,1)} %get-tuple-element.52.x_ref.refs_0_, ...), custom_call_target="tpu_custom_call" | custom-call | tf_op jit(solution)/shard_map/forward/pallas_call | solution.py:311
  161.0 14.7 %backward.2 = (f32[128,576]{1,0:T(8,128)}, bf16[128,640]{1,0:T(8,128)(2,1)}, bf16[2,1024,384]{2,1,0:T(8,128)(2,1)}, f32[1,576]{1,0:T(1,128)}, bf16[2,4,4,576,384]{4,3,2,1,0:T(8,128)(2,1)}) custom-call(bf16[128,576]{1,0:T(8,128)(2,1)} %bitcast.111, f32[128,576]{1,0:T(8,128)} %get-tuple-element.55.h_ref, bf16[6,192,1024]{2,1,0:T(8,128)(2,1)} %get-tuple-element.56.p_ref, ...), custom_call_target="tpu_custom_call" | custom-call | tf_op jit(solution)/shard_map/backward/pallas_call | solution.py:416
  175.6 21.0 %dkv.2 = (bf16[128,576]{1,0:T(8,128)(2,1)}, f32[1,576]{1,0:T(1,128)}, bf16[2,4,4,576,384]{4,3,2,1,0:T(8,128)(2,1)}) custom-call(bf16[2,4,4,64,384]{4,3,2,1,0:T(8,128)(2,1)} %bitcast.105, bf16[128,576]{1,0:T(8,128)(2,1)} %get-tuple-element.61.n1_ref, bf16[128,640]{1,0:T(8,128)(2,1)} %get-tuple-element.62.dq_ref, ...), custom_call_target="tpu_custom_call", output_to_operand_aliasing={{2}: (10, {})} | custom-call | tf_op jit(solution)/shard_map/dkv/pallas_call | solution.py:514
  196.7 14.8 %backward.3 = (f32[128,576]{1,0:T(8,128)}, bf16[128,640]{1,0:T(8,128)(2,1)}, bf16[2,1024,384]{2,1,0:T(8,128)(2,1)}, f32[1,576]{1,0:T(1,128)}, bf16[2,4,4,576,384]{4,3,2,1,0:T(8,128)(2,1)}) custom-call(bf16[128,576]{1,0:T(8,128)(2,1)} %get-tuple-element.66.dy_ref, f32[128,576]{1,0:T(8,128)} %get-tuple-element.67.h_ref, ...), custom_call_target="tpu_custom_call", output_to_operand_aliasing={{4}: (12, {})} | custom-call | tf_op jit(solution)/shard_map/backward/pallas_call | solution.py:416
  211.5 0.0 copy-start.2
  211.5 0.0 copy-start.3
  211.5 0.0 copy-start.4
  211.5 0.0 copy-start.6
  211.5 0.0 copy-start.7
  211.5 0.0 copy-start.8
  211.5 21.0 %dkv.3 = (bf16[128,576]{1,0:T(8,128)(2,1)}, f32[1,576]{1,0:T(1,128)}, bf16[2,4,4,576,384]{4,3,2,1,0:T(8,128)(2,1)}) custom-call(bf16[2,4,4,64,384]{4,3,2,1,0:T(8,128)(2,1)} %bitcast.104, bf16[128,576]{1,0:T(8,128)(2,1)} %get-tuple-element.74.n1_ref, bf16[128,640]{1,0:T(8,128)(2,1)} %get-tuple-element.75.dq_ref, ...), custom_call_target="tpu_custom_call", output_to_operand_aliasing={{2}: (10, {})} | custom-call | tf_op jit(solution)/shard_map/dkv/pallas_call | solution.py:514
  232.5 0.0 copy-done.2
  232.5 1.0 maximum_bitcast_fusion
  233.5 0.0 copy-start
  233.5 0.0 copy-done.3
  233.5 0.0 copy-done.4
  233.5 0.1 maximum_bitcast_fusion.1
  233.6 0.6 copy-done
  234.2 0.9 pad_maximum_fusion.pairs
  235.1 0.0 copy-done.1
  235.1 0.1 pad.9.clone
  235.2 0.7 maximum_bitcast_fusion.2
  236.0 0.6 pad_maximum_fusion.5.gains
  236.6 96.8 %reduce.1 = (bf16[4,4,144,384]{3,2,1,0:T(8,128)(2,1)}, f32[8,576]{1,0:T(8,128)}, bf16[2,128,576]{2,1,0:T(8,128)(2,1)}) custom-call(bf16[2,4,4,576,384]{4,3,2,1,0:T(8,128)(2,1)} %get-tuple-element.81.grads, f32[2,8,576]{2,1,0:T(8,128)} %pad_maximum_fusion.5.gains, bf16[2,2,128,576]{3,2,1,0:T(8,128)(2,1)} %pad_maximum_fusion.pairs), custom_call_target="tpu_custom_call" | custom-call | tf_op jit(solution)/shard_map/reduce/pallas_call | solution.py:645
  333.4 1.7 convert_bitcast_fusion
  335.1 0.4 copy.67
  335.5 1.6 slice_bitcast_fusion
  337.0 0.7 slice.75
  337.7 2.0 reshape.137
  339.7 2.3 fusion.7
  342.0 1.8 copy.61
  343.8 1.7 copy.63
  345.5 1.8 copy.62
  347.2 1.7 copy.64
  348.9 1.0 slice_bitcast_fusion.3
  349.9 1.1 fusion.2
  351.0 1.0 broadcast_select_fusion
  352.0 0.9 fusion.3
  353.0 1.4 fusion.8
  (15 shorter events, 0.1 us)
Async XLA Ops:
  1.6 9.3 %copy-start.5 = (s32[2,1024]{1,0:T(2,128)}, s32[2,1024]{1,0:T(2,128)S(1)}, u32[]{:S(2)}) copy-start(s32[2,1024]{1,0:T(2,128)S(1)} %broadcast_add_fusion.refs_4_) | copy-start | bytes 24580
  10.9 71.0 %copy-start.9 = (bf16[1,144]{1,0:T(2,128)(2,1)S(1)}, bf16[1,144]{1,0:T(2,128)(2,1)}, u32[]{:S(2)}) copy-start(bf16[1,144]{1,0:T(2,128)(2,1)} %param.20) | copy-start | bytes 868
  10.9 71.0 %copy-start.10 = (bf16[1,144]{1,0:T(2,128)(2,1)S(1)}, bf16[1,144]{1,0:T(2,128)(2,1)}, u32[]{:S(2)}) copy-start(bf16[1,144]{1,0:T(2,128)(2,1)} %param.15) | copy-start | bytes 868
  211.5 21.0 %copy-start.2 = (bf16[128,576]{1,0:T(8,128)(2,1)S(1)}, bf16[128,576]{1,0:T(8,128)(2,1)}, u32[]{:S(2)}) copy-start(bf16[128,576]{1,0:T(8,128)(2,1)} %get-tuple-element.52.x_ref.refs_0_) | copy-start | bytes 442372
  211.5 22.0 %copy-start.3 = (bf16[128,576]{1,0:T(8,128)(2,1)S(1)}, bf16[128,576]{1,0:T(8,128)(2,1)}, u32[]{:S(2)}) copy-start(bf16[128,576]{1,0:T(8,128)(2,1)} %get-tuple-element.66.dy_ref) | copy-start | bytes 442372
  211.5 22.0 %copy-start.4 = (bf16[128,576]{1,0:T(8,128)(2,1)S(1)}, bf16[128,576]{1,0:T(8,128)(2,1)}, u32[]{:S(2)}) copy-start(bf16[128,576]{1,0:T(8,128)(2,1)} %get-tuple-element.80) | copy-start | bytes 442372
  211.5 23.7 %copy-start.6 = (f32[1,576]{1,0:T(1,128)S(1)}, f32[1,576]{1,0:T(1,128)}, u32[]{:S(2)}) copy-start(f32[1,576]{1,0:T(1,128)} %get-tuple-element.85) | copy-start | bytes 6916
  211.5 23.7 %copy-start.7 = (f32[1,576]{1,0:T(1,128)S(1)}, f32[1,576]{1,0:T(1,128)}, u32[]{:S(2)}) copy-start(f32[1,576]{1,0:T(1,128)} %get-tuple-element.84) | copy-start | bytes 6916
  211.5 23.7 %copy-start.8 = (f32[1,576]{1,0:T(1,128)S(1)}, f32[1,576]{1,0:T(1,128)}, u32[]{:S(2)}) copy-start(f32[1,576]{1,0:T(1,128)} %get-tuple-element.83) | copy-start | bytes 6916
  233.5 0.7 copy-start
  234.2 0.9 copy-start.1
